TPU v7x, 32 devices: a whole 2x2x4 slice. The times are simulated.
32 devices in a mesh: section: 4 (over z), mp: 8 (over y, x, core).
Axes of the slice: x: 2, y: 2, z: 4, core: 2. Of those that a mesh axis runs over, the one named last changes fastest.
Arguments:
- entering_hidden: bfloat16 [4, 256, 8192], P('section', None, 'mp'), may hold values from -12 to 12
- section_weight: bfloat16 [4, 8192, 8192], P('section', None, 'mp'), may hold values from -0.0625 to 0.0625
- section_norm_gain: bfloat16 [4, 8192], P('section', 'mp'), may hold values from 0.5 to 1.5
- plugin_narrowing_factors: bfloat16 [4, 8, 8192, 64], P('section', 'mp'), may hold values from -0.0625 to 0.0625
- plugin_widening_factors: bfloat16 [4, 8, 64, 8192], P('section', 'mp'), may hold values from -0.75 to 0.75
- reward_head: bfloat16 [8192], P('mp'), may hold values from -0.0625 to 0.0625
- adapter_of_block: int32 [4, 2], replicated, may hold values from 0 to 7
- live_block_rows: int32 [4, 2], P('section'), may hold values from 1 to 128
Outputs:
- hidden_out: bfloat16 [4, 256, 8192], P('section', None, 'mp')
- scores: float32 [4, 256], P('section')
All inputs are finite; a program needn't handle non-finite values.
Results may differ from a plain program's by a relative error of at most 0.022.
Values may be sent and summed in bfloat16 or wider, within the bound.
No kernel may reach another device: no remote copies, remote signals or barrier semaphores. Data moves between devices by JAX's collectives and lax.ppermute only.
A program may use at most 64 MiB of HBM per device.

v0:
```python
import functools

import jax
import jax.numpy as jnp
from jax import lax
from jax.experimental import pallas as pl
from jax.experimental.pallas import tpu as pltpu
from jax.sharding import PartitionSpec as P

BLOCK = 128
SIDE = 128
LAG = 2
SPAN = 1

VMEM = pl.BlockSpec(memory_space=pltpu.VMEM)
SMEM = pl.BlockSpec(memory_space=pltpu.SMEM)


def near(x):
    return pltpu.with_memory_space_constraint(x, pltpu.VMEM)


def call(kernel, out_shape, args, name, flops, moved, limit=8, after=()):
    info, *arrays = args
    count = len(arrays)

    def body(info_ref, *refs):
        kernel(info_ref, *refs[:count], *refs[count + len(after) :])

    return pl.pallas_call(
        body,
        out_shape=out_shape,
        in_specs=[SMEM] + [VMEM] * count + [pl.BlockSpec(memory_space=pl.ANY)] * len(after),
        out_specs=jax.tree.map(lambda _: VMEM, out_shape),
        compiler_params=pltpu.CompilerParams(vmem_limit_bytes=limit << 20),
        cost_estimate=pl.CostEstimate(flops=flops, bytes_accessed=moved, transcendentals=0),
        name=name,
    )(info, *map(near, arrays), *after)


def tie(x, after):
    def body(*_):
        pass

    return pl.pallas_call(
        body,
        out_shape=pltpu.VMEM(x.shape, x.dtype),
        in_specs=[VMEM] + [pl.BlockSpec(memory_space=pl.ANY)] * len(after),
        out_specs=VMEM,
        input_output_aliases={0: 0},
        compiler_params=pltpu.CompilerParams(vmem_limit_bytes=1 << 20),
        cost_estimate=pl.CostEstimate(flops=0, bytes_accessed=0, transcendentals=0),
        name="tie",
    )(near(x), *after)


def adapter_at(info_ref, owners, owned, tick, chunks, block):
    mine = jnp.clip(tick - LAG * info_ref[0], 0, chunks - 1)
    adapter = info_ref[2 + owners + mine * SPAN + block]
    if owned == 1:
        return adapter ^ info_ref[1]
    return (lax.div(adapter, owned) ^ info_ref[1]) * owned + lax.rem(adapter, owned)


def prep_kernel(rank, owners, owned, tick, chunks, block, info_ref, *refs):
    *sources, gain_ref, down_ref, x_ref, m_ref = refs
    copies = m_ref.shape[0]
    rows, piece = x_ref.shape
    picked = [source[b * rows : (b + 1) * rows, :].astype(jnp.float32) for source, b in zip(sources, block)]
    x = jnp.where(info_ref[0] == 0, *picked) if len(picked) == 2 else picked[0]
    x_ref[...] = x.astype(jnp.bfloat16)
    scaled = (x * gain_ref[...].astype(jnp.float32)).astype(jnp.bfloat16)
    squares = jnp.sum(x * x, axis=1, keepdims=True)
    high = squares.astype(jnp.bfloat16).astype(jnp.float32)
    low = squares - high
    lane = lax.broadcasted_iota(jnp.int32, (rows, SIDE), 1)
    inner = []
    for b in range(SPAN):
        product = lax.dot_general(
            scaled[b * BLOCK : (b + 1) * BLOCK],
            down_ref[adapter_at(info_ref, owners, owned, tick, chunks, b)],
            (((1,), (1,)), ((), ())),
            preferred_element_type=jnp.float32,
        )
        inner.append(jnp.concatenate([product, jnp.zeros((BLOCK, SIDE - rank), jnp.float32)], axis=1))
    inner = jnp.concatenate(inner, axis=0) if SPAN > 1 else inner[0]
    side = jnp.where(lane == rank, high, jnp.where(lane == rank + 1, low, inner)).astype(jnp.bfloat16)
    for copy in range(copies):
        m_ref[copy, :, :piece] = scaled
        m_ref[copy, :, piece:] = side


def stage_kernel(w_ref, *refs):
    *_, o_ref, sem = refs
    copy = pltpu.make_async_copy(w_ref, o_ref, sem)
    copy.start()
    copy.wait()


def staged(weight, after):
    return pl.pallas_call(
        stage_kernel,
        out_shape=pltpu.VMEM(weight.shape, weight.dtype),
        in_specs=[pl.BlockSpec(memory_space=pl.ANY)] * (1 + len(after)),
        out_specs=VMEM,
        scratch_shapes=[pltpu.SemaphoreType.DMA],
        compiler_params=pltpu.CompilerParams(vmem_limit_bytes=4 << 20),
        cost_estimate=pl.CostEstimate(flops=0, bytes_accessed=2 * weight.size, transcendentals=0),
        name="stage",
    )(pltpu.with_memory_space_constraint(weight, pltpu.HBM), *after)


def layer_kernel(rank, owners, owned, tick, chunks, counts, info_ref, *refs):
    *parts, w_ref, x_ref, up_ref, o_ref = refs
    rows, piece = x_ref.shape
    width = w_ref.shape[0]
    side = jnp.zeros((rows, SIDE), jnp.float32)
    for part, count in zip(parts, counts):
        for k in range(count):
            side = side + part[k, :, piece:].astype(jnp.float32)
    squares = side[:, rank : rank + 1] + side[:, rank + 1 : rank + 2]
    scale = lax.rsqrt(squares / width + 1e-05)
    inner = (2.0 * side[:, :rank]).astype(jnp.bfloat16)
    tile = min(piece, 256)

    @pl.loop(0, piece // tile)
    def _(n):
        columns = pl.ds(pl.multiple_of(n * tile, tile), tile)
        delta = [
            jnp.dot(
                inner[b * BLOCK : (b + 1) * BLOCK],
                up_ref[adapter_at(info_ref, owners, owned, tick, chunks, b), :, columns],
                preferred_element_type=jnp.float32,
            )
            for b in range(SPAN)
        ]
        total = jnp.concatenate(delta, axis=0) if SPAN > 1 else delta[0]
        i = 0
        for part, count in zip(parts, counts):
            for k in range(count):
                depth = pl.ds(pl.multiple_of(info_ref[2 + i] * piece, piece), piece)
                total += jnp.dot(
                    part[k, :, :piece], w_ref[depth, columns], preferred_element_type=jnp.float32
                )
                i += 1
        h = x_ref[:, columns].astype(jnp.float32)
        o_ref[:, columns] = (h + scale * total).astype(jnp.bfloat16)


def cut_kernel(owners, info_ref, maps_ref, *outs):
    piece = outs[0].shape[2]
    for k, out in enumerate(outs):
        out[...] = maps_ref[:, :, pl.ds(pl.multiple_of((info_ref[1] ^ k) * piece, piece), piece)]


def stack_kernel(info_ref, *refs):
    *blocks, o_ref = refs
    owned = blocks[0].shape[0]
    for i, block in enumerate(blocks):
        o_ref[i * owned : (i + 1) * owned] = block[...]


def join_kernel(info_ref, *refs):
    *blocks, o_ref = refs
    rows = blocks[0].shape[0]
    for i, block in enumerate(blocks):
        o_ref[i * rows : (i + 1) * rows, :] = block[...]


def finish_kernel(sections, info_ref, *refs):
    *blocks, head_ref, o_ref, score_ref = refs
    for section in range(sections):

        @pl.when(info_ref[0] == section)
        def _():
            h = blocks[section][...]
            o_ref[...] = h
            score_ref[...] = jnp.sum(
                h.astype(jnp.float32) * head_ref[...].astype(jnp.float32), axis=1, keepdims=True
            )


def shards(
    entering_hidden,
    section_weight,
    section_norm_gain,
    plugin_narrowing_factors,
    plugin_widening_factors,
    reward_head,
    adapter_of_block,
    live_block_rows,
):
    sections = lax.axis_size("section")
    section = lax.axis_index("section")
    chips = lax.axis_size("chip")
    cores = lax.axis_size("core")
    owners = chips * cores
    everyone = ("chip", "core")
    batches_here, rows, piece = entering_hidden.shape
    micro = batches_here * sections
    span = BLOCK * SPAN
    per_micro = rows // span
    owned = plugin_narrowing_factors.shape[1]
    rank = plugin_narrowing_factors.shape[3]
    chunks = micro * per_micro
    pairwise = chips == 4 and cores == 2

    chip, core = lax.axis_index("chip"), lax.axis_index("core")
    if pairwise:
        near_by, far = jnp.where(core == 0, 1, 2), jnp.where(core == 0, 2, 1)
        place = chip * cores + core
        parts = [(0, 0), (0, 1), (near_by, 0), (near_by, 1), (3, 0), (far, 1), (far, 0), (3, 1)]
        order = [(chip ^ there) * cores + (core ^ other) for there, other in parts]
    else:
        place = jnp.zeros_like(core)
        order = [i * cores + (core + k) % cores for k in range(cores) for i in range(chips)]
    info = jnp.concatenate([jnp.stack([section, place] + order), adapter_of_block.reshape(-1)])
    info = info.astype(jnp.int32)

    def spread(maps, after):
        if not pairwise:
            maps = jnp.moveaxis(maps.reshape(owned, rank, owners, piece), 2, 0)
            maps = lax.all_to_all(maps, everyone, split_axis=0, concat_axis=0, tiled=True)
            return maps.reshape(owners * owned, rank, piece), after
        out_shape = [pltpu.VMEM((owned, rank, piece), maps.dtype) for _ in range(owners)]
        size = 2 * maps.size
        blocks = list(call(functools.partial(cut_kernel, owners), out_shape, (info, maps), "cut", 0, 2 * size, after=after))
        mine = blocks[:1]
        for k in range(1, owners):
            blocks[k] = lax.ppermute(blocks[k], everyone, [(i, i ^ k) for i in range(owners)])
        out_shape = pltpu.VMEM((owners * owned, rank, piece), maps.dtype)
        return call(stack_kernel, out_shape, (info, *blocks), "stack", 0, 2 * size), mine

    down, cut = spread(jnp.swapaxes(plugin_narrowing_factors[0], 1, 2), ())
    weight = staged(section_weight[0], cut)

    feeds = []
    for m in range(micro):
        home, slot = divmod(m, batches_here)
        block = entering_hidden[slot]
        feeds.append(block if home == 0 else lax.ppermute(block, "section", [(home, 0)]))

    def over_cores(part):
        return [
            lax.ppermute(part, "core", [((c + k) % cores, c) for c in range(cores)]) for k in range(1, cores)
        ]

    def over_chips(part, steps):
        pairs = [(i * cores + c, (i ^ steps[c]) * cores + c) for i in range(chips) for c in range(cores)]
        return lax.ppermute(part, everyone, pairs)

    def gather_start(message):
        if not pairwise:
            parts = lax.all_to_all(message, "chip", split_axis=0, concat_axis=0, tiled=True)
            return [parts] + over_cores(parts)
        first = over_chips(message, (1, 2))
        (other,) = over_cores(message)
        second = over_chips(other, (1, 2))
        return [message, other, first, second]

    def gather_end(parts, after):
        if not pairwise:
            return parts
        message, other, first, second = parts
        first = tie(first, after) if after else first
        third = over_chips(first, (2, 1))
        return [message, other, first, second, third] + [
            swapped for part in (first, second, third) for swapped in over_cores(part)
        ]

    def prep(tick, sources, blocks, after):
        out_shape = (
            pltpu.VMEM((span, piece), jnp.bfloat16),
            pltpu.VMEM((1 if pairwise else chips, span, piece + SIDE), jnp.bfloat16),
        )
        kernel = functools.partial(prep_kernel, rank, owners, owned, tick, chunks, blocks)
        args = (info, *sources, section_norm_gain, down)
        return call(kernel, out_shape, args, "prep", 2 * span * piece * SIDE, span * piece * 8, after=after)

    def layer(tick, parts, x, after):
        counts = tuple(part.shape[0] for part in parts)
        width = piece * owners
        kernel = functools.partial(layer_kernel, rank, owners, owned, tick, chunks, counts)
        args = (info, *parts, weight, x, up)
        out_shape = pltpu.VMEM((span, piece), jnp.bfloat16)
        return call(kernel, out_shape, args, "layer", 2 * span * width * piece, 2 * width * piece, after=after)

    arrived, state, hs, done, home_blocks, returned = {}, {}, {}, {}, {}, {}
    ticks = chunks + LAG * (sections - 1)

    def active(tick):
        return [s for s in range(sections) if 0 <= tick - LAG * s < chunks]

    def begin(tick):
        sources, blocks = [], []
        if 0 in active(tick):
            m, b = divmod(tick, per_micro)
            sources.append(feeds[m])
            blocks.append(b)
        if active(tick) != [0]:
            sources.append(arrived.pop(tick))
            blocks.append(0)
        if tick == 0:
            after = [weight]
        elif LAG == 2:
            after = [state[tick - 1][2][4 if pairwise else 0]]
        else:
            after = [hs[tick - 2]] if tick >= 2 else []
        x, message = prep(tick, sources, blocks, after)
        state[tick] = [x, message, gather_start(message)]

    begin(0)
    state[0][2] = gather_end(state[0][2], [])
    up, _ = spread(plugin_widening_factors[0], (state[0][1],))
    for tick in range(ticks):
        after = []
        if tick + 1 < ticks:
            begin(tick + 1)
            after.append(state[tick + 1][1])
        if tick in returned:
            after.append(returned.pop(tick))
        x, _, parts = state.pop(tick)
        h = hs[tick] = layer(tick, parts, x, after)
        if tick + 1 < ticks:
            state[tick + 1][2] = gather_end(state[tick + 1][2], [h])
        onward = [(s, s + 1) for s in active(tick) if s + 1 < sections]
        if onward:
            arrived[tick + LAG] = lax.ppermute(h, "section", onward)
        if sections - 1 in active(tick):
            last = tick - LAG * (sections - 1)
            done[last] = h
            if last % per_micro == per_micro - 1:
                m = last // per_micro
                block = [done[m * per_micro + b] for b in range(per_micro)]
                if per_micro > 1:
                    out_shape = pltpu.VMEM((rows, piece), jnp.bfloat16)
                    block = call(join_kernel, out_shape, (info, *block), "join", 0, rows * piece * 4)
                else:
                    block = block[0]
                home = m // batches_here
                if home != sections - 1:
                    block = lax.ppermute(block, "section", [(sections - 1, home)])
                    returned[tick + 2] = block
                home_blocks[m] = block

    hidden, partial_score = [], []
    for slot in range(batches_here):
        out_shape = (
            jax.ShapeDtypeStruct((rows, piece), jnp.bfloat16),
            jax.ShapeDtypeStruct((rows, 1), jnp.float32),
        )
        block = [home_blocks[home * batches_here + slot] for home in range(sections)]
        kernel = functools.partial(finish_kernel, sections)
        args = (info, *block, reward_head[None])
        h, s = call(kernel, out_shape, args, "finish", 2 * rows * piece, rows * piece * 4)
        hidden.append(h)
        partial_score.append(s[:, 0])
    raw = lax.psum(jnp.stack(partial_score), everyone)
    place = jnp.arange(rows, dtype=jnp.int32) % BLOCK
    limits = jnp.repeat(live_block_rows, BLOCK, axis=1)
    scores = jnp.where(place[None, :] < limits, raw, jnp.float32(0.0))
    return (jnp.stack(hidden), scores)


def solution(mesh):
    sections, owners = mesh.shape["section"], mesh.shape["mp"]
    cores = 2 if owners % 2 == 0 else 1
    fine = jax.sharding.Mesh(
        mesh.devices.reshape(sections, owners // cores, cores), ("section", "chip", "core")
    )
    mp = ("chip", "core")
    placed = (
        P("section", None, mp),
        P("section", None, mp),
        P("section", mp),
        P("section", mp, None, None),
        P("section", mp, None, None),
        P(mp),
        P(),
        P("section", None),
    )
    return jax.shard_map(
        shards,
        mesh=fine,
        in_specs=placed,
        out_specs=(P("section", None, mp), P("section", None)),
        check_vma=False,
    )
```

profile of v0, /device:TPU:16, one launch (start us, length us, event | category | flops | bytes accessed | tf_op | source)
XLA Modules:
  0.0 315.3 jit_solution(3653467117307535383)
XLA Ops:
  11.2 5.8 %stage.1.refs_3_.refs_8_ = bf16[8192,1024]{1,0:T(8,128)(2,1)S(1)} custom-call(bf16[8192,1024]{1,0:T(8,128)(2,1)} %bitcast.26, bf16[1,64,1024]{2,1,0:T(8,128)(2,1)S(1)} %get-tuple-element.48.refs_0_), custom_call_target="tpu_custom_call" | custom-call | bytes 16777216 | tf_op jit(solution)/shard_map/stage/pallas_call | solution.py:101
  23.6 4.0 %collective-permute-done.11.refs_2_ = bf16[1,128,1152]{2,1,0:T(8,128)(2,1)S(1)} collective-permute-done((bf16[1,128,1152]{2,1,0:T(8,128)(2,1)S(1)}, bf16[1,128,1152]{2,1,0:T(8,128)(2,1)S(1)}, u32[]{:S(2)}, u32[]{:S(2)}) %collective-permute-start.11) | collective-permute-done | bytes 294944 | tf_op jit(solution)/shard_map/ppermute | solution.py:250
  32.2 4.1 %collective-permute-done.18.refs_2_ = bf16[1,64,1024]{2,1,0:T(8,128)(2,1)S(1)} collective-permute-done((bf16[1,64,1024]{2,1,0:T(8,128)(2,1)S(1)}, bf16[1,64,1024]{2,1,0:T(8,128)(2,1)S(1)}, u32[]{:S(2)}, u32[]{:S(2)}) %collective-permute-start.18) | collective-permute-done | bytes 131104 | tf_op jit(solution)/shard_map/ppermute | solution.py:230
  51.0 4.0 %layer.14.__1_ = bf16[128,1024]{1,0:T(8,128)(2,1)S(1)} custom-call(s32[18]{0:T(128)S(1)} %concatenate.3.info_ref, bf16[1,128,1152]{2,1,0:T(8,128)(2,1)S(1)} %get-tuple-element.56.refs_1_.refs_0_, bf16[1,128,1152]{2,1,0:T(8,128)(2,1)S(1)} %collective-permute-done.10.refs_1_, bf16[1,128,1152]{2,1,0:T(8,128)(2,1)S(1)} %collective-permute-done.11.refs_2_, ...), custom_call_target="tpu_custom_call" | custom-call | flops 2147483648 | bytes 16777216 | tf_op jit(solution)/shard_map/layer/pallas_call | solution.py:30
  58.8 5.6 %collective-permute-done.26.refs_4_ = bf16[1,128,1152]{2,1,0:T(8,128)(2,1)S(1)} collective-permute-done((bf16[1,128,1152]{2,1,0:T(8,128)(2,1)S(1)}, bf16[1,128,1152]{2,1,0:T(8,128)(2,1)S(1)}, u32[]{:S(2)}, u32[]{:S(2)}) %collective-permute-start.26) | collective-permute-done | bytes 294944 | tf_op jit(solution)/shard_map/ppermute | solution.py:250
  67.5 4.0 %layer.15.__1_ = bf16[128,1024]{1,0:T(8,128)(2,1)S(1)} custom-call(s32[18]{0:T(128)S(1)} %concatenate.3.info_ref, bf16[1,128,1152]{2,1,0:T(8,128)(2,1)S(1)} %get-tuple-element.66.refs_11_.refs_0_, bf16[1,128,1152]{2,1,0:T(8,128)(2,1)S(1)} %collective-permute-done.29.refs_1_, bf16[1,128,1152]{2,1,0:T(8,128)(2,1)S(1)} %tie.13.refs_2_, ...), custom_call_target="tpu_custom_call" | custom-call | flops 2147483648 | bytes 16777216 | tf_op jit(solution)/shard_map/layer/pallas_call | solution.py:30
  76.2 5.8 %collective-permute-done.35.refs_4_ = bf16[1,128,1152]{2,1,0:T(8,128)(2,1)S(1)} collective-permute-done((bf16[1,128,1152]{2,1,0:T(8,128)(2,1)S(1)}, bf16[1,128,1152]{2,1,0:T(8,128)(2,1)S(1)}, u32[]{:S(2)}, u32[]{:S(2)}) %collective-permute-start.35) | collective-permute-done | bytes 294944 | tf_op jit(solution)/shard_map/ppermute | solution.py:250
  84.4 5.6 %collective-permute-start.1 = (bf16[256,1024]{1,0:T(8,128)(2,1)S(1)}, bf16[256,1024]{1,0:T(8,128)(2,1)S(1)}, u32[]{:S(2)}, u32[]{:S(2)}) collective-permute-start(bf16[256,1024]{1,0:T(8,128)(2,1)S(1)} %bitcast.22), channel_id=1, source_target_pairs={{16,0},{17,1},{18,2},{19,3},{20,4},{21,5},{22,6},{23,7}} | collective-permute-start | bytes 1572872 | tf_op jit(solution)/shard_map/ppermute | solution.py:241
  90.1 4.0 %layer.16.__1_ = bf16[128,1024]{1,0:T(8,128)(2,1)S(1)} custom-call(s32[18]{0:T(128)S(1)} %concatenate.3.info_ref, bf16[1,128,1152]{2,1,0:T(8,128)(2,1)S(1)} %get-tuple-element.67.refs_11_.refs_0_, bf16[1,128,1152]{2,1,0:T(8,128)(2,1)S(1)} %collective-permute-done.27.refs_1_, bf16[1,128,1152]{2,1,0:T(8,128)(2,1)S(1)} %tie.14.refs_2_, ...), custom_call_target="tpu_custom_call" | custom-call | flops 2147483648 | bytes 16777216 | tf_op jit(solution)/shard_map/layer/pallas_call | solution.py:30
  97.9 5.9 %collective-permute-done.42.refs_4_ = bf16[1,128,1152]{2,1,0:T(8,128)(2,1)S(1)} collective-permute-done((bf16[1,128,1152]{2,1,0:T(8,128)(2,1)S(1)}, bf16[1,128,1152]{2,1,0:T(8,128)(2,1)S(1)}, u32[]{:S(2)}, u32[]{:S(2)}) %collective-permute-start.42) | collective-permute-done | bytes 294944 | tf_op jit(solution)/shard_map/ppermute | solution.py:250
  108.1 4.0 %layer.17.__1_ = bf16[128,1024]{1,0:T(8,128)(2,1)S(1)} custom-call(s32[18]{0:T(128)S(1)} %concatenate.3.info_ref, bf16[1,128,1152]{2,1,0:T(8,128)(2,1)S(1)} %get-tuple-element.70.refs_11_.refs_0_, bf16[1,128,1152]{2,1,0:T(8,128)(2,1)S(1)} %collective-permute-done.45.refs_1_, bf16[1,128,1152]{2,1,0:T(8,128)(2,1)S(1)} %tie.15.refs_2_, ...), custom_call_target="tpu_custom_call" | custom-call | flops 2147483648 | bytes 16777216 | tf_op jit(solution)/shard_map/layer/pallas_call | solution.py:30
  116.9 5.6 %collective-permute-done.51.refs_4_ = bf16[1,128,1152]{2,1,0:T(8,128)(2,1)S(1)} collective-permute-done((bf16[1,128,1152]{2,1,0:T(8,128)(2,1)S(1)}, bf16[1,128,1152]{2,1,0:T(8,128)(2,1)S(1)}, u32[]{:S(2)}, u32[]{:S(2)}) %collective-permute-start.51) | collective-permute-done | bytes 294944 | tf_op jit(solution)/shard_map/ppermute | solution.py:250
  126.6 4.0 %layer.18.__1_ = bf16[128,1024]{1,0:T(8,128)(2,1)S(1)} custom-call(s32[18]{0:T(128)S(1)} %concatenate.3.info_ref, bf16[1,128,1152]{2,1,0:T(8,128)(2,1)S(1)} %get-tuple-element.71.refs_11_.refs_0_, bf16[1,128,1152]{2,1,0:T(8,128)(2,1)S(1)} %collective-permute-done.43.refs_1_, bf16[1,128,1152]{2,1,0:T(8,128)(2,1)S(1)} %tie.16.refs_2_, ...), custom_call_target="tpu_custom_call" | custom-call | flops 2147483648 | bytes 16777216 | tf_op jit(solution)/shard_map/layer/pallas_call | solution.py:30
  137.0 4.0 %collective-permute-done.58.refs_4_ = bf16[1,128,1152]{2,1,0:T(8,128)(2,1)S(1)} collective-permute-done((bf16[1,128,1152]{2,1,0:T(8,128)(2,1)S(1)}, bf16[1,128,1152]{2,1,0:T(8,128)(2,1)S(1)}, u32[]{:S(2)}, u32[]{:S(2)}) %collective-permute-start.58) | collective-permute-done | bytes 294944 | tf_op jit(solution)/shard_map/ppermute | solution.py:250
  144.8 4.0 %layer.19.__1_ = bf16[128,1024]{1,0:T(8,128)(2,1)S(1)} custom-call(s32[18]{0:T(128)S(1)} %concatenate.3.info_ref, bf16[1,128,1152]{2,1,0:T(8,128)(2,1)S(1)} %get-tuple-element.74.refs_11_.refs_0_, bf16[1,128,1152]{2,1,0:T(8,128)(2,1)S(1)} %collective-permute-done.61.refs_1_, bf16[1,128,1152]{2,1,0:T(8,128)(2,1)S(1)} %tie.17.refs_2_, ...), custom_call_target="tpu_custom_call" | custom-call | flops 2147483648 | bytes 16777216 | tf_op jit(solution)/shard_map/layer/pallas_call | solution.py:30
  162.6 4.0 %layer.20.__1_.refs_0_ = bf16[128,1024]{1,0:T(8,128)(2,1)S(1)} custom-call(s32[18]{0:T(128)S(1)} %concatenate.3.info_ref, bf16[1,128,1152]{2,1,0:T(8,128)(2,1)S(1)} %get-tuple-element.75.refs_11_.refs_0_, bf16[1,128,1152]{2,1,0:T(8,128)(2,1)S(1)} %collective-permute-done.59.refs_1_, bf16[1,128,1152]{2,1,0:T(8,128)(2,1)S(1)} %tie.18.refs_2_, ...), custom_call_target="tpu_custom_call" | custom-call | flops 2147483648 | bytes 16777216 | tf_op jit(solution)/shard_map/layer/pallas_call | solution.py:30
  180.9 4.0 %layer.21.refs_1_.__1_ = bf16[128,1024]{1,0:T(8,128)(2,1)S(1)} custom-call(s32[18]{0:T(128)S(1)} %concatenate.3.info_ref, bf16[1,128,1152]{2,1,0:T(8,128)(2,1)S(1)} %get-tuple-element.78.refs_11_.refs_0_, bf16[1,128,1152]{2,1,0:T(8,128)(2,1)S(1)} %collective-permute-done.72.refs_1_, bf16[1,128,1152]{2,1,0:T(8,128)(2,1)S(1)} %tie.19.refs_2_, ...), custom_call_target="tpu_custom_call" | custom-call | flops 2147483648 | bytes 16777216 | tf_op jit(solution)/shard_map/layer/pallas_call | solution.py:30
  191.8 3.5 %collective-permute-done.84.refs_3_.refs_4_ = bf16[1,128,1152]{2,1,0:T(8,128)(2,1)S(1)} collective-permute-done((bf16[1,128,1152]{2,1,0:T(8,128)(2,1)S(1)}, bf16[1,128,1152]{2,1,0:T(8,128)(2,1)S(1)}, u32[]{:S(2)}, u32[]{:S(2)}) %collective-permute-start.84) | collective-permute-done | bytes 294944 | tf_op jit(solution)/shard_map/ppermute | solution.py:250
  200.0 4.0 %layer.22.__1_.refs_0_ = bf16[128,1024]{1,0:T(8,128)(2,1)S(1)} custom-call(s32[18]{0:T(128)S(1)} %concatenate.3.info_ref, bf16[1,128,1152]{2,1,0:T(8,128)(2,1)S(1)} %get-tuple-element.80.refs_11_.refs_0_, bf16[1,128,1152]{2,1,0:T(8,128)(2,1)S(1)} %collective-permute-done.81.refs_1_, bf16[1,128,1152]{2,1,0:T(8,128)(2,1)S(1)} %tie.20.refs_2_, ...), custom_call_target="tpu_custom_call" | custom-call | flops 2147483648 | bytes 16777216 | tf_op jit(solution)/shard_map/layer/pallas_call | solution.py:30
  206.7 3.8 %collective-permute-start.96 = (bf16[128,1024]{1,0:T(8,128)(2,1)S(1)}, bf16[128,1024]{1,0:T(8,128)(2,1)S(1)}, u32[]{:S(2)}, u32[]{:S(2)}) collective-permute-start(bf16[128,1024]{1,0:T(8,128)(2,1)S(1)} %layer.22.__1_.refs_0_), channel_id=1, source_target_pairs={{8,16},{16,24},{9,17},{17,25},{10,18},{18,26},{11,19},{19,27},{12,... | collective-permute-start | bytes 786440 | tf_op jit(solution)/shard_map/ppermute | solution.py:328
  210.6 3.8 %collective-permute-done.92.refs_3_.refs_4_ = bf16[1,128,1152]{2,1,0:T(8,128)(2,1)S(1)} collective-permute-done((bf16[1,128,1152]{2,1,0:T(8,128)(2,1)S(1)}, bf16[1,128,1152]{2,1,0:T(8,128)(2,1)S(1)}, u32[]{:S(2)}, u32[]{:S(2)}) %collective-permute-start.92) | collective-permute-done | bytes 294944 | tf_op jit(solution)/shard_map/ppermute | solution.py:250
  218.3 4.0 %layer.23.refs_1_.__1_ = bf16[128,1024]{1,0:T(8,128)(2,1)S(1)} custom-call(s32[18]{0:T(128)S(1)} %concatenate.3.info_ref, bf16[1,128,1152]{2,1,0:T(8,128)(2,1)S(1)} %get-tuple-element.82.refs_11_.refs_0_, bf16[1,128,1152]{2,1,0:T(8,128)(2,1)S(1)} %collective-permute-done.89.refs_1_, bf16[1,128,1152]{2,1,0:T(8,128)(2,1)S(1)} %tie.21.refs_2_, ...), custom_call_target="tpu_custom_call" | custom-call | flops 2147483648 | bytes 16777216 | tf_op jit(solution)/shard_map/layer/pallas_call | solution.py:30
  225.8 4.0 %collective-permute-start.105 = (bf16[128,1024]{1,0:T(8,128)(2,1)S(1)}, bf16[128,1024]{1,0:T(8,128)(2,1)S(1)}, u32[]{:S(2)}, u32[]{:S(2)}) collective-permute-start(bf16[128,1024]{1,0:T(8,128)(2,1)S(1)} %layer.23.refs_1_.__1_), channel_id=1, source_target_pairs={{8,16},{16,24},{9,17},{17,25},{10,18},{18,26},{11,19},{19,27},{12,... | collective-permute-start | bytes 786440 | tf_op jit(solution)/shard_map/ppermute | solution.py:328
  237.4 4.0 %layer.24.__1_.refs_0_ = bf16[128,1024]{1,0:T(8,128)(2,1)S(1)} custom-call(s32[18]{0:T(128)S(1)} %concatenate.3.info_ref, bf16[1,128,1152]{2,1,0:T(8,128)(2,1)S(1)} %get-tuple-element.84.refs_11_.refs_0_, bf16[1,128,1152]{2,1,0:T(8,128)(2,1)S(1)} %collective-permute-done.98.refs_1_, bf16[1,128,1152]{2,1,0:T(8,128)(2,1)S(1)} %tie.22.refs_2_, ...), custom_call_target="tpu_custom_call" | custom-call | flops 2147483648 | bytes 16777216 | tf_op jit(solution)/shard_map/layer/pallas_call | solution.py:30
  244.1 4.5 %collective-permute-start.113 = (bf16[128,1024]{1,0:T(8,128)(2,1)S(1)}, bf16[128,1024]{1,0:T(8,128)(2,1)S(1)}, u32[]{:S(2)}, u32[]{:S(2)}) collective-permute-start(bf16[128,1024]{1,0:T(8,128)(2,1)S(1)} %layer.24.__1_.refs_0_), channel_id=1, source_target_pairs={{16,24},{17,25},{18,26},{19,27},{20,28},{21,29},{22,30},{23,31}} | collective-permute-start | bytes 786440 | tf_op jit(solution)/shard_map/ppermute | solution.py:328
  256.0 4.0 %layer.25.refs_1_.__1_ = bf16[128,1024]{1,0:T(8,128)(2,1)S(1)} custom-call(s32[18]{0:T(128)S(1)} %concatenate.3.info_ref, bf16[1,128,1152]{2,1,0:T(8,128)(2,1)S(1)} %get-tuple-element.86.refs_11_.refs_0_, bf16[1,128,1152]{2,1,0:T(8,128)(2,1)S(1)} %collective-permute-done.106.refs_1_, bf16[1,128,1152]{2,1,0:T(8,128)(2,1)S(1)} %tie.23.refs_2_, ...), custom_call_target="tpu_custom_call" | custom-call | flops 2147483648 | bytes 16777216 | tf_op jit(solution)/shard_map/layer/pallas_call | solution.py:30
  263.4 4.6 %collective-permute-start.122 = (bf16[128,1024]{1,0:T(8,128)(2,1)S(1)}, bf16[128,1024]{1,0:T(8,128)(2,1)S(1)}, u32[]{:S(2)}, u32[]{:S(2)}) collective-permute-start(bf16[128,1024]{1,0:T(8,128)(2,1)S(1)} %layer.25.refs_1_.__1_), channel_id=1, source_target_pairs={{16,24},{17,25},{18,26},{19,27},{20,28},{21,29},{22,30},{23,31}} | collective-permute-start | bytes 786440 | tf_op jit(solution)/shard_map/ppermute | solution.py:328
  273.8 4.0 %layer.26.__1_.refs_0_ = bf16[128,1024]{1,0:T(8,128)(2,1)S(1)} custom-call(s32[18]{0:T(128)S(1)} %concatenate.3.info_ref, bf16[1,128,1152]{2,1,0:T(8,128)(2,1)S(1)} %get-tuple-element.88.refs_11_.refs_0_, bf16[1,128,1152]{2,1,0:T(8,128)(2,1)S(1)} %collective-permute-done.115.refs_1_, bf16[1,128,1152]{2,1,0:T(8,128)(2,1)S(1)} %tie.24.refs_2_, ...), custom_call_target="tpu_custom_call" | custom-call | flops 2147483648 | bytes 16777216 | tf_op jit(solution)/shard_map/layer/pallas_call | solution.py:30
  283.7 4.5 %collective-permute-done.126.refs_4_ = bf16[1,128,1152]{2,1,0:T(8,128)(2,1)S(1)} collective-permute-done((bf16[1,128,1152]{2,1,0:T(8,128)(2,1)S(1)}, bf16[1,128,1152]{2,1,0:T(8,128)(2,1)S(1)}, u32[]{:S(2)}, u32[]{:S(2)}) %collective-permute-start.126) | collective-permute-done | bytes 294944 | tf_op jit(solution)/shard_map/ppermute | solution.py:250
  288.7 8.0 %collective-permute-done.114.refs_11_.refs_2_ = bf16[256,1024]{1,0:T(8,128)(2,1)S(1)} collective-permute-done((bf16[256,1024]{1,0:T(8,128)(2,1)S(1)}, bf16[256,1024]{1,0:T(8,128)(2,1)S(1)}, u32[]{:S(2)}, u32[]{:S(2)}) %collective-permute-start.114) | collective-permute-done | bytes 524320 | tf_op jit(solution)/shard_map/ppermute | solution.py:342
  296.7 4.0 %layer.27.refs_1_ = bf16[128,1024]{1,0:T(8,128)(2,1)S(1)} custom-call(s32[18]{0:T(128)S(1)} %concatenate.3.info_ref, bf16[1,128,1152]{2,1,0:T(8,128)(2,1)S(1)} %get-tuple-element.90.refs_11_.refs_0_, bf16[1,128,1152]{2,1,0:T(8,128)(2,1)S(1)} %collective-permute-done.123.refs_1_, bf16[1,128,1152]{2,1,0:T(8,128)(2,1)S(1)} %tie.25.refs_2_, ...), custom_call_target="tpu_custom_call" | custom-call | flops 2147483648 | bytes 16777216 | tf_op jit(solution)/shard_map/layer/pallas_call | solution.py:30
  302.9 11.8 %psum.7 = f32[1,256]{1,0:T(1,128)S(1)} all-reduce(f32[1,256]{1,0:T(1,128)S(1)} %bitcast.27), channel_id=1, replica_groups=mesh['section'=4,'chip'=4,'core'=2] {'chip','core'}, use_global_device_ids=true, to_apply=%region_0.1 | all-reduce | flops 256 | bytes 2048 | tf_op jit(solution)/shard_map/psum | solution.py:358
  (299 shorter events, 163.1 us)
Async XLA Ops:
  5.1 11.9 %collective-permute-start.5 = (bf16[1,64,1024]{2,1,0:T(8,128)(2,1)S(1)}, bf16[1,64,1024]{2,1,0:T(8,128)(2,1)S(1)}, u32[]{:S(2)}, u32[]{:S(2)}) collective-permute-start(bf16[1,64,1024]{2,1,0:T(8,128)(2,1)S(1)} %get-tuple-element.51), channel_id=1, source_target_pairs={{0,3},{1,2},{2,1},{3,0},{4,7},{5,6},{6,5},{7,4},{8,11},{9,10},{10,... | collective-permute-start | bytes 393224 | tf_op jit(solution)/shard_map/ppermute | solution.py:230
  5.4 11.6 %collective-permute-start.6 = (bf16[1,64,1024]{2,1,0:T(8,128)(2,1)S(1)}, bf16[1,64,1024]{2,1,0:T(8,128)(2,1)S(1)}, u32[]{:S(2)}, u32[]{:S(2)}) collective-permute-start(bf16[1,64,1024]{2,1,0:T(8,128)(2,1)S(1)} %get-tuple-element.52), channel_id=1, source_target_pairs={{0,4},{1,5},{2,6},{3,7},{4,0},{5,1},{6,2},{7,3},{8,12},{9,13},{10,... | collective-permute-start | bytes 393224 | tf_op jit(solution)/shard_map/ppermute | solution.py:230
  6.9 12.1 %collective-permute-start.7 = (bf16[1,64,1024]{2,1,0:T(8,128)(2,1)S(1)}, bf16[1,64,1024]{2,1,0:T(8,128)(2,1)S(1)}, u32[]{:S(2)}, u32[]{:S(2)}) collective-permute-start(bf16[1,64,1024]{2,1,0:T(8,128)(2,1)S(1)} %get-tuple-element.53), channel_id=1, source_target_pairs={{0,5},{1,4},{2,7},{3,6},{4,1},{5,0},{6,3},{7,2},{8,13},{9,12},{10,... | collective-permute-start | bytes 393224 | tf_op jit(solution)/shard_map/ppermute | solution.py:230
  7.1 11.9 %collective-permute-start.8 = (bf16[1,64,1024]{2,1,0:T(8,128)(2,1)S(1)}, bf16[1,64,1024]{2,1,0:T(8,128)(2,1)S(1)}, u32[]{:S(2)}, u32[]{:S(2)}) collective-permute-start(bf16[1,64,1024]{2,1,0:T(8,128)(2,1)S(1)} %get-tuple-element.54), channel_id=1, source_target_pairs={{0,6},{1,7},{2,4},{3,5},{4,2},{5,3},{6,0},{7,1},{8,14},{9,15},{10,... | collective-permute-start | bytes 393224 | tf_op jit(solution)/shard_map/ppermute | solution.py:230
  9.9 9.1 %collective-permute-start.9 = (bf16[1,64,1024]{2,1,0:T(8,128)(2,1)S(1)}, bf16[1,64,1024]{2,1,0:T(8,128)(2,1)S(1)}, u32[]{:S(2)}, u32[]{:S(2)}) collective-permute-start(bf16[1,64,1024]{2,1,0:T(8,128)(2,1)S(1)} %get-tuple-element.55), channel_id=1, source_target_pairs={{0,7},{1,6},{2,5},{3,4},{4,3},{5,2},{6,1},{7,0},{8,15},{9,14},{10,... | collective-permute-start | bytes 393224 | tf_op jit(solution)/shard_map/ppermute | solution.py:230
  22.4 17.2 %collective-permute-start.12 = (bf16[1,128,1152]{2,1,0:T(8,128)(2,1)S(1)}, bf16[1,128,1152]{2,1,0:T(8,128)(2,1)S(1)}, u32[]{:S(2)}, u32[]{:S(2)}) collective-permute-start(bf16[1,128,1152]{2,1,0:T(8,128)(2,1)S(1)} %collective-permute-done.10.refs_1_), channel_id=1, source_target_pairs={{0,2},{1,5},{2,0},{3,7},{4,6},{5,1},{6,4},{7,3},{8,10},{9,13},{10,... | collective-permute-start | bytes 884744 | tf_op jit(solution)/shard_map/ppermute | solution.py:250
  27.6 12.5 %collective-permute-start.13 = (bf16[1,128,1152]{2,1,0:T(8,128)(2,1)S(1)}, bf16[1,128,1152]{2,1,0:T(8,128)(2,1)S(1)}, u32[]{:S(2)}, u32[]{:S(2)}) collective-permute-start(bf16[1,128,1152]{2,1,0:T(8,128)(2,1)S(1)} %collective-permute-done.11.refs_2_), channel_id=1, source_target_pairs={{0,4},{1,3},{2,6},{3,1},{4,0},{5,7},{6,2},{7,5},{8,12},{9,11},{10,... | collective-permute-start | bytes 884744 | tf_op jit(solution)/shard_map/ppermute | solution.py:250
  39.6 10.7 %collective-permute-start.14 = (bf16[1,128,1152]{2,1,0:T(8,128)(2,1)S(1)}, bf16[1,128,1152]{2,1,0:T(8,128)(2,1)S(1)}, u32[]{:S(2)}, u32[]{:S(2)}) collective-permute-start(bf16[1,128,1152]{2,1,0:T(8,128)(2,1)S(1)} %collective-permute-done.11.refs_2_), channel_id=1, source_target_pairs={{1,0},{0,1},{3,2},{2,3},{5,4},{4,5},{7,6},{6,7},{9,8},{8,9},{11,10... | collective-permute-start | bytes 884744 | tf_op jit(solution)/shard_map/ppermute | solution.py:245
  39.6 11.4 %collective-permute-start.15 = (bf16[1,128,1152]{2,1,0:T(8,128)(2,1)S(1)}, bf16[1,128,1152]{2,1,0:T(8,128)(2,1)S(1)}, u32[]{:S(2)}, u32[]{:S(2)}) collective-permute-start(bf16[1,128,1152]{2,1,0:T(8,128)(2,1)S(1)} %collective-permute-done.12.refs_3_), channel_id=1, source_target_pairs={{1,0},{0,1},{3,2},{2,3},{5,4},{4,5},{7,6},{6,7},{9,8},{8,9},{11,10... | collective-permute-start | bytes 884744 | tf_op jit(solution)/shard_map/ppermute | solution.py:245
  40.1 10.9 %collective-permute-start.16 = (bf16[1,128,1152]{2,1,0:T(8,128)(2,1)S(1)}, bf16[1,128,1152]{2,1,0:T(8,128)(2,1)S(1)}, u32[]{:S(2)}, u32[]{:S(2)}) collective-permute-start(bf16[1,128,1152]{2,1,0:T(8,128)(2,1)S(1)} %collective-permute-done.13.refs_3_.refs_4_), channel_id=1, source_target_pairs={{1,0},{0,1},{3,2},{2,3},{5,4},{4,5},{7,6},{6,7},{9,8},{8,9},{11,10... | collective-permute-start | bytes 884744 | tf_op jit(solution)/shard_map/ppermute | solution.py:245
  50.3 14.7 %collective-permute-start.2 = (bf16[256,1024]{1,0:T(8,128)(2,1)S(1)}, bf16[256,1024]{1,0:T(8,128)(2,1)S(1)}, u32[]{:S(2)}, u32[]{:S(2)}) collective-permute-start(bf16[256,1024]{1,0:T(8,128)(2,1)S(1)} %bitcast.21), channel_id=1, source_target_pairs={{8,0},{9,1},{10,2},{11,3},{12,4},{13,5},{14,6},{15,7}} | collective-permute-start | bytes 1572872 | tf_op jit(solution)/shard_map/ppermute | solution.py:241
  55.0 9.4 %collective-permute-start.26 = (bf16[1,128,1152]{2,1,0:T(8,128)(2,1)S(1)}, bf16[1,128,1152]{2,1,0:T(8,128)(2,1)S(1)}, u32[]{:S(2)}, u32[]{:S(2)}) collective-permute-start(bf16[1,128,1152]{2,1,0:T(8,128)(2,1)S(1)} %tie.13.refs_2_), channel_id=1, source_target_pairs={{0,4},{1,3},{2,6},{3,1},{4,0},{5,7},{6,2},{7,5},{8,12},{9,11},{10,... | collective-permute-start | bytes 884744 | tf_op jit(solution)/shard_map/ppermute | solution.py:250
  58.7 8.8 %collective-permute-start.31 = (bf16[1,128,1152]{2,1,0:T(8,128)(2,1)S(1)}, bf16[1,128,1152]{2,1,0:T(8,128)(2,1)S(1)}, u32[]{:S(2)}, u32[]{:S(2)}) collective-permute-start(bf16[1,128,1152]{2,1,0:T(8,128)(2,1)S(1)} %tie.13.refs_2_), channel_id=1, source_target_pairs={{1,0},{0,1},{3,2},{2,3},{5,4},{4,5},{7,6},{6,7},{9,8},{8,9},{11,10... | collective-permute-start | bytes 884744 | tf_op jit(solution)/shard_map/ppermute | solution.py:245
  72.5 9.5 %collective-permute-start.35 = (bf16[1,128,1152]{2,1,0:T(8,128)(2,1)S(1)}, bf16[1,128,1152]{2,1,0:T(8,128)(2,1)S(1)}, u32[]{:S(2)}, u32[]{:S(2)}) collective-permute-start(bf16[1,128,1152]{2,1,0:T(8,128)(2,1)S(1)} %tie.14.refs_2_), channel_id=1, source_target_pairs={{0,4},{1,3},{2,6},{3,1},{4,0},{5,7},{6,2},{7,5},{8,12},{9,11},{10,... | collective-permute-start | bytes 884744 | tf_op jit(solution)/shard_map/ppermute | solution.py:250
  83.3 10.7 %collective-permute-start.41 = (bf16[1,128,1152]{2,1,0:T(8,128)(2,1)S(1)}, bf16[1,128,1152]{2,1,0:T(8,128)(2,1)S(1)}, u32[]{:S(2)}, u32[]{:S(2)}) collective-permute-start(bf16[1,128,1152]{2,1,0:T(8,128)(2,1)S(1)} %get-tuple-element.70.refs_11_.refs_0_), channel_id=1, source_target_pairs={{0,2},{1,5},{2,0},{3,7},{4,6},{5,1},{6,4},{7,3},{8,10},{9,13},{10,... | collective-permute-start | bytes 884744 | tf_op jit(solution)/shard_map/ppermute | solution.py:250
  84.1 11.3 %collective-permute-start.45 = (bf16[1,128,1152]{2,1,0:T(8,128)(2,1)S(1)}, bf16[1,128,1152]{2,1,0:T(8,128)(2,1)S(1)}, u32[]{:S(2)}, u32[]{:S(2)}) collective-permute-start(bf16[1,128,1152]{2,1,0:T(8,128)(2,1)S(1)} %get-tuple-element.70.refs_11_.refs_0_), channel_id=1, source_target_pairs={{1,0},{0,1},{3,2},{2,3},{5,4},{4,5},{7,6},{6,7},{9,8},{8,9},{11,10... | collective-permute-start | bytes 884744 | tf_op jit(solution)/shard_map/ppermute | solution.py:245
  84.4 20.0 %collective-permute-start.1 = (bf16[256,1024]{1,0:T(8,128)(2,1)S(1)}, bf16[256,1024]{1,0:T(8,128)(2,1)S(1)}, u32[]{:S(2)}, u32[]{:S(2)}) collective-permute-start(bf16[256,1024]{1,0:T(8,128)(2,1)S(1)} %bitcast.22), channel_id=1, source_target_pairs={{16,0},{17,1},{18,2},{19,3},{20,4},{21,5},{22,6},{23,7}} | collective-permute-start | bytes 1572872 | tf_op jit(solution)/shard_map/ppermute | solution.py:241
  94.1 9.8 %collective-permute-start.42 = (bf16[1,128,1152]{2,1,0:T(8,128)(2,1)S(1)}, bf16[1,128,1152]{2,1,0:T(8,128)(2,1)S(1)}, u32[]{:S(2)}, u32[]{:S(2)}) collective-permute-start(bf16[1,128,1152]{2,1,0:T(8,128)(2,1)S(1)} %tie.15.refs_2_), channel_id=1, source_target_pairs={{0,4},{1,3},{2,6},{3,1},{4,0},{5,7},{6,2},{7,5},{8,12},{9,11},{10,... | collective-permute-start | bytes 884744 | tf_op jit(solution)/shard_map/ppermute | solution.py:250
  96.6 9.8 %collective-permute-start.40 = (bf16[128,1024]{1,0:T(8,128)(2,1)S(1)}, bf16[128,1024]{1,0:T(8,128)(2,1)S(1)}, u32[]{:S(2)}, u32[]{:S(2)}) collective-permute-start(bf16[128,1024]{1,0:T(8,128)(2,1)S(1)} %layer.16.__1_), channel_id=1, source_target_pairs={{0,8},{8,16},{1,9},{9,17},{2,10},{10,18},{3,11},{11,19},{4,12},{12... | collective-permute-start | bytes 786440 | tf_op jit(solution)/shard_map/ppermute | solution.py:328
  97.9 10.2 %collective-permute-start.47 = (bf16[1,128,1152]{2,1,0:T(8,128)(2,1)S(1)}, bf16[1,128,1152]{2,1,0:T(8,128)(2,1)S(1)}, u32[]{:S(2)}, u32[]{:S(2)}) collective-permute-start(bf16[1,128,1152]{2,1,0:T(8,128)(2,1)S(1)} %tie.15.refs_2_), channel_id=1, source_target_pairs={{1,0},{0,1},{3,2},{2,3},{5,4},{4,5},{7,6},{6,7},{9,8},{8,9},{11,10... | collective-permute-start | bytes 884744 | tf_op jit(solution)/shard_map/ppermute | solution.py:245
  116.8 9.0 %collective-permute-start.52 = (bf16[1,128,1152]{2,1,0:T(8,128)(2,1)S(1)}, bf16[1,128,1152]{2,1,0:T(8,128)(2,1)S(1)}, u32[]{:S(2)}, u32[]{:S(2)}) collective-permute-start(bf16[1,128,1152]{2,1,0:T(8,128)(2,1)S(1)} %tie.16.refs_2_), channel_id=1, source_target_pairs={{1,0},{0,1},{3,2},{2,3},{5,4},{4,5},{7,6},{6,7},{9,8},{8,9},{11,10... | collective-permute-start | bytes 884744 | tf_op jit(solution)/shard_map/ppermute | solution.py:245
  125.8 15.6 %collective-permute-start = (bf16[256,1024]{1,0:T(8,128)(2,1)S(1)}, bf16[256,1024]{1,0:T(8,128)(2,1)S(1)}, u32[]{:S(2)}, u32[]{:S(2)}) collective-permute-start(bf16[256,1024]{1,0:T(8,128)(2,1)S(1)} %bitcast.23), channel_id=1, source_target_pairs={{24,0},{25,1},{26,2},{27,3},{28,4},{29,5},{30,6},{31,7}} | collective-permute-start | bytes 1572872 | tf_op jit(solution)/shard_map/ppermute | solution.py:241
  131.7 9.2 %collective-permute-start.58 = (bf16[1,128,1152]{2,1,0:T(8,128)(2,1)S(1)}, bf16[1,128,1152]{2,1,0:T(8,128)(2,1)S(1)}, u32[]{:S(2)}, u32[]{:S(2)}) collective-permute-start(bf16[1,128,1152]{2,1,0:T(8,128)(2,1)S(1)} %tie.17.refs_2_), channel_id=1, source_target_pairs={{0,4},{1,3},{2,6},{3,1},{4,0},{5,7},{6,2},{7,5},{8,12},{9,11},{10,... | collective-permute-start | bytes 884744 | tf_op jit(solution)/shard_map/ppermute | solution.py:250
  133.8 9.3 %collective-permute-start.56 = (bf16[128,1024]{1,0:T(8,128)(2,1)S(1)}, bf16[128,1024]{1,0:T(8,128)(2,1)S(1)}, u32[]{:S(2)}, u32[]{:S(2)}) collective-permute-start(bf16[128,1024]{1,0:T(8,128)(2,1)S(1)} %layer.18.__1_), channel_id=1, source_target_pairs={{0,8},{8,16},{16,24},{1,9},{9,17},{17,25},{2,10},{10,18},{18,26},{... | collective-permute-start | bytes 786440 | tf_op jit(solution)/shard_map/ppermute | solution.py:328
  199.3 19.0 %collective-permute-start.80 = (bf16[256,1024]{1,0:T(8,128)(2,1)S(1)}, bf16[256,1024]{1,0:T(8,128)(2,1)S(1)}, u32[]{:S(2)}, u32[]{:S(2)}) collective-permute-start(bf16[256,1024]{1,0:T(8,128)(2,1)S(1)} %join.4), channel_id=1, source_target_pairs={{24,0},{25,1},{26,2},{27,3},{28,4},{29,5},{30,6},{31,7}} | collective-permute-start | bytes 1572872 | tf_op jit(solution)/shard_map/ppermute | solution.py:342
  204.6 9.8 %collective-permute-start.92 = (bf16[1,128,1152]{2,1,0:T(8,128)(2,1)S(1)}, bf16[1,128,1152]{2,1,0:T(8,128)(2,1)S(1)}, u32[]{:S(2)}, u32[]{:S(2)}) collective-permute-start(bf16[1,128,1152]{2,1,0:T(8,128)(2,1)S(1)} %tie.21.refs_2_), channel_id=1, source_target_pairs={{0,4},{1,3},{2,6},{3,1},{4,0},{5,7},{6,2},{7,5},{8,12},{9,11},{10,... | collective-permute-start | bytes 884744 | tf_op jit(solution)/shard_map/ppermute | solution.py:250
  206.7 9.9 %collective-permute-start.96 = (bf16[128,1024]{1,0:T(8,128)(2,1)S(1)}, bf16[128,1024]{1,0:T(8,128)(2,1)S(1)}, u32[]{:S(2)}, u32[]{:S(2)}) collective-permute-start(bf16[128,1024]{1,0:T(8,128)(2,1)S(1)} %layer.22.__1_.refs_0_), channel_id=1, source_target_pairs={{8,16},{16,24},{9,17},{17,25},{10,18},{18,26},{11,19},{19,27},{12,... | collective-permute-start | bytes 786440 | tf_op jit(solution)/shard_map/ppermute | solution.py:328
  236.7 19.2 %collective-permute-start.97 = (bf16[256,1024]{1,0:T(8,128)(2,1)S(1)}, bf16[256,1024]{1,0:T(8,128)(2,1)S(1)}, u32[]{:S(2)}, u32[]{:S(2)}) collective-permute-start(bf16[256,1024]{1,0:T(8,128)(2,1)S(1)} %join.5), channel_id=1, source_target_pairs={{24,8},{25,9},{26,10},{27,11},{28,12},{29,13},{30,14},{31,15}} | collective-permute-start | bytes 1572872 | tf_op jit(solution)/shard_map/ppermute | solution.py:342
  241.9 9.8 %collective-permute-start.109 = (bf16[1,128,1152]{2,1,0:T(8,128)(2,1)S(1)}, bf16[1,128,1152]{2,1,0:T(8,128)(2,1)S(1)}, u32[]{:S(2)}, u32[]{:S(2)}) collective-permute-start(bf16[1,128,1152]{2,1,0:T(8,128)(2,1)S(1)} %tie.23.refs_2_), channel_id=1, source_target_pairs={{0,4},{1,3},{2,6},{3,1},{4,0},{5,7},{6,2},{7,5},{8,12},{9,11},{10,... | collective-permute-start | bytes 884744 | tf_op jit(solution)/shard_map/ppermute | solution.py:250
  244.1 10.1 %collective-permute-start.113 = (bf16[128,1024]{1,0:T(8,128)(2,1)S(1)}, bf16[128,1024]{1,0:T(8,128)(2,1)S(1)}, u32[]{:S(2)}, u32[]{:S(2)}) collective-permute-start(bf16[128,1024]{1,0:T(8,128)(2,1)S(1)} %layer.24.__1_.refs_0_), channel_id=1, source_target_pairs={{16,24},{17,25},{18,26},{19,27},{20,28},{21,29},{22,30},{23,31}} | collective-permute-start | bytes 786440 | tf_op jit(solution)/shard_map/ppermute | solution.py:328
  282.3 14.3 %collective-permute-start.114 = (bf16[256,1024]{1,0:T(8,128)(2,1)S(1)}, bf16[256,1024]{1,0:T(8,128)(2,1)S(1)}, u32[]{:S(2)}, u32[]{:S(2)}) collective-permute-start(bf16[256,1024]{1,0:T(8,128)(2,1)S(1)} %join.6), channel_id=1, source_target_pairs={{24,16},{25,17},{26,18},{27,19},{28,20},{29,21},{30,22},{31,23}} | collective-permute-start | bytes 1572872 | tf_op jit(solution)/shard_map/ppermute | solution.py:342
  283.6 13.0 %collective-permute-start.127 = (bf16[1,128,1152]{2,1,0:T(8,128)(2,1)S(1)}, bf16[1,128,1152]{2,1,0:T(8,128)(2,1)S(1)}, u32[]{:S(2)}, u32[]{:S(2)}) collective-permute-start(bf16[1,128,1152]{2,1,0:T(8,128)(2,1)S(1)} %tie.25.refs_2_), channel_id=1, source_target_pairs={{1,0},{0,1},{3,2},{2,3},{5,4},{4,5},{7,6},{6,7},{9,8},{8,9},{11,10... | collective-permute-start | bytes 884744 | tf_op jit(solution)/shard_map/ppermute | solution.py:245
  (104 other events, 738.0 us)
where the time goes:
time: 316 us; the launch traced here: 315 us
  starting transfers between devices  114 us (36%)
  waiting for transfers between devices  106 us (34%)
  Pallas kernels  79.1 us (25%)
  blocking collectives  11.8 us (4%)
    ppermute x42, waiting for transfers between devices, over_chips(): return lax.ppermute(part, everyone, pairs)  73.5 us
    pallas_call x37, Pallas kernels, call(): pl.pallas_call(body, out_shape=out_shape, in_specs=[SMEM] + [VMEM] * coun...  73.2 us
    ppermute x42, starting transfers between devices, over_chips(): return lax.ppermute(part, everyone, pairs)  44.6 us
    ppermute x12, starting transfers between devices, shards(): arrived[tick + LAG] = lax.ppermute(h, 'section', onward)  33.9 us
    ppermute x14, starting transfers between devices, spread(): lax.ppermute(blocks[k], everyone, [(i, i ^ k) for i in range(owners)])  16.3 us
    ppermute x12, waiting for transfers between devices, shards(): arrived[tick + LAG] = lax.ppermute(h, 'section', onward)  14.6 us
    psum x1, blocking collectives, shards(): raw = lax.psum(jnp.stack(partial_score), everyone)  11.8 us
    ppermute x14, waiting for transfers between devices, spread(): lax.ppermute(blocks[k], everyone, [(i, i ^ k) for i in range(owners)])  10.1 us
  transfers between devices with their start and end apart: 130, of which 43 were waited for; matrix products, arithmetic and copies ran while one was open for 0% of the time, Pallas kernels for 23%

commit v1 on v0

--- a/solution.py
+++ b/solution.py
@@ -110,14 +110,42 @@
     )(pltpu.with_memory_space_constraint(weight, pltpu.HBM), *after)
 
 
-def layer_kernel(rank, owners, owned, tick, chunks, counts, info_ref, *refs):
-    *parts, w_ref, x_ref, up_ref, o_ref = refs
-    rows, piece = x_ref.shape
+def piece_dots(info_ref, w_ref, parts, starts, columns):
+    total = None
+    for part, start in zip(parts, starts):
+        piece = w_ref.shape[1]
+        for k in range(part.shape[0]):
+            depth = pl.ds(pl.multiple_of(info_ref[2 + start + k] * piece, piece), piece)
+            term = jnp.dot(part[k, :, :piece], w_ref[depth, columns], preferred_element_type=jnp.float32)
+            total = term if total is None else total + term
+    return total
+
+
+def side_sum(parts, piece):
+    return sum(part[k, :, piece:].astype(jnp.float32) for part in parts for k in range(part.shape[0]))
+
+
+def layer_a_kernel(starts, seeded, info_ref, *refs):
+    *parts, w_ref, total_ref, side_ref = refs
+    if seeded:
+        *parts, old_total, old_side = parts
+    piece = w_ref.shape[1]
+    side = side_sum(parts, piece)
+    side_ref[...] = old_side[...] + side if seeded else side
+    tile = min(piece, 256)
+
+    @pl.loop(0, piece // tile)
+    def _(n):
+        columns = pl.ds(pl.multiple_of(n * tile, tile), tile)
+        total = piece_dots(info_ref, w_ref, parts, starts, columns)
+        total_ref[:, columns] = old_total[:, columns] + total if seeded else total
+
+
+def layer_b_kernel(rank, owners, owned, tick, chunks, starts, info_ref, *refs):
+    *parts, w_ref, x_ref, up_ref, total_ref, side_ref, o_ref = refs
+    piece = x_ref.shape[1]
     width = w_ref.shape[0]
-    side = jnp.zeros((rows, SIDE), jnp.float32)
-    for part, count in zip(parts, counts):
-        for k in range(count):
-            side = side + part[k, :, piece:].astype(jnp.float32)
+    side = side_ref[...] + side_sum(parts, piece)
     squares = side[:, rank : rank + 1] + side[:, rank + 1 : rank + 2]
     scale = lax.rsqrt(squares / width + 1e-05)
     inner = (2.0 * side[:, :rank]).astype(jnp.bfloat16)
@@ -135,16 +163,50 @@
             for b in range(SPAN)
         ]
         total = jnp.concatenate(delta, axis=0) if SPAN > 1 else delta[0]
-        i = 0
-        for part, count in zip(parts, counts):
-            for k in range(count):
-                depth = pl.ds(pl.multiple_of(info_ref[2 + i] * piece, piece), piece)
-                total += jnp.dot(
-                    part[k, :, :piece], w_ref[depth, columns], preferred_element_type=jnp.float32
-                )
-                i += 1
+        total += total_ref[:, columns] + piece_dots(info_ref, w_ref, parts, starts, columns)
         h = x_ref[:, columns].astype(jnp.float32)
         o_ref[:, columns] = (h + scale * total).astype(jnp.bfloat16)
+
+
+def join_kernel(info_ref, *refs):
+    *blocks, o_ref = refs
+    rows = blocks[0].shape[0]
+    for i, block in enumerate(blocks):
+        o_ref[i * rows : (i + 1) * rows, :] = block[...]
+
+
+def finish_kernel(sections, counts, info_ref, *refs):
+    *blocks, head_ref, o_ref, score_ref = refs
+    taken = 0
+    for section, count in zip(range(sections), counts):
+        own = blocks[taken : taken + count]
+        taken += count
+
+        @pl.when(info_ref[0] == section)
+        def _():
+            row = 0
+            for block in own:
+                span = block.shape[0]
+                h = block[...]
+                o_ref[row : row + span, :] = h
+                score_ref[:, row : row + span] = lax.dot_general(
+                    head_ref[...], h, (((1,), (1,)), ((), ())), preferred_element_type=jnp.float32
+                )
+                row += span
+
+
+def add_kernel(info_ref, *refs):
+    *terms, o_ref = refs
+    o_ref[...] = sum(term[...] for term in terms)
+
+
+def score_kernel(info_ref, limits_ref, *refs):
+    *terms, o_ref = refs
+    total = sum(term[...] for term in terms)
+    lane = lax.broadcasted_iota(jnp.int32, (1, BLOCK), 1)
+    for b in range(total.shape[1] // BLOCK):
+        columns = slice(b * BLOCK, (b + 1) * BLOCK)
+        o_ref[:, columns] = jnp.where(lane < limits_ref[:, b : b + 1], total[:, columns], 0.0)
 
 
 def cut_kernel(owners, info_ref, maps_ref, *outs):
@@ -158,26 +220,6 @@
     owned = blocks[0].shape[0]
     for i, block in enumerate(blocks):
         o_ref[i * owned : (i + 1) * owned] = block[...]
-
-
-def join_kernel(info_ref, *refs):
-    *blocks, o_ref = refs
-    rows = blocks[0].shape[0]
-    for i, block in enumerate(blocks):
-        o_ref[i * rows : (i + 1) * rows, :] = block[...]
-
-
-def finish_kernel(sections, info_ref, *refs):
-    *blocks, head_ref, o_ref, score_ref = refs
-    for section in range(sections):
-
-        @pl.when(info_ref[0] == section)
-        def _():
-            h = blocks[section][...]
-            o_ref[...] = h
-            score_ref[...] = jnp.sum(
-                h.astype(jnp.float32) * head_ref[...].astype(jnp.float32), axis=1, keepdims=True
-            )
 
 
 def shards(
@@ -260,13 +302,12 @@
 
     def gather_end(parts, after):
         if not pairwise:
-            return parts
-        message, other, first, second = parts
+            return [], [(part, chips * (1 + k)) for k, part in enumerate(parts[1:])]
+        _, _, first, second = parts
         first = tie(first, after) if after else first
         third = over_chips(first, (2, 1))
-        return [message, other, first, second, third] + [
-            swapped for part in (first, second, third) for swapped in over_cores(part)
-        ]
+        swapped = [over_cores(part)[0] for part in (first, second, third)]
+        return [(first, 2), (second, 3), (swapped[0], 5), (swapped[1], 6)], [(third, 4), (swapped[2], 7)]
 
     def prep(tick, sources, blocks, after):
         out_shape = (
@@ -277,15 +318,23 @@
         args = (info, *sources, section_norm_gain, down)
         return call(kernel, out_shape, args, "prep", 2 * span * piece * SIDE, span * piece * 8, after=after)
 
-    def layer(tick, parts, x, after):
-        counts = tuple(part.shape[0] for part in parts)
+    def layer_a(parts, seed, after):
         width = piece * owners
-        kernel = functools.partial(layer_kernel, rank, owners, owned, tick, chunks, counts)
-        args = (info, *parts, weight, x, up)
+        kernel = functools.partial(layer_a_kernel, [start for _, start in parts], bool(seed))
+        out_shape = (pltpu.VMEM((span, piece), jnp.float32), pltpu.VMEM((span, SIDE), jnp.float32))
+        args = (info, *[part for part, _ in parts], *seed, weight)
+        return call(kernel, out_shape, args, "layer_a", span * width * piece, width * piece, after=after)
+
+    def layer_b(tick, parts, x, sums, after):
+        width = piece * owners
+        kernel = functools.partial(
+            layer_b_kernel, rank, owners, owned, tick, chunks, [start for _, start in parts]
+        )
+        args = (info, *[part for part, _ in parts], weight, x, up, *sums)
         out_shape = pltpu.VMEM((span, piece), jnp.bfloat16)
-        return call(kernel, out_shape, args, "layer", 2 * span * width * piece, 2 * width * piece, after=after)
-
-    arrived, state, hs, done, home_blocks, returned = {}, {}, {}, {}, {}, {}
+        return call(kernel, out_shape, args, "layer_b", span * width * piece // 2, width * piece // 2, after=after)
+
+    arrived, state, sums, done, home_blocks, returned = {}, {}, {}, {}, {}, {}
     ticks = chunks + LAG * (sections - 1)
 
     def active(tick):
@@ -302,27 +351,37 @@
             blocks.append(0)
         if tick == 0:
             after = [weight]
-        elif LAG == 2:
-            after = [state[tick - 1][2][4 if pairwise else 0]]
         else:
-            after = [hs[tick - 2]] if tick >= 2 else []
+            after = [sums[tick - 1][1]]
         x, message = prep(tick, sources, blocks, after)
         state[tick] = [x, message, gather_start(message)]
 
+    def own_chip(tick, after):
+        parts = state[tick][2]
+        own = [(parts[0], 0), (parts[1], 1)] if pairwise else [(parts[0], 0)]
+        sums[tick] = layer_a(own, (), after)
+        state[tick][2:] = gather_end(parts, [sums[tick][1]] if after else [])
+
+    def near_chips(tick, after):
+        if state[tick][2]:
+            sums[tick] = layer_a(state[tick][2], sums[tick], after)
+
+    up, _ = spread(plugin_widening_factors[0], (weight,))
     begin(0)
-    state[0][2] = gather_end(state[0][2], [])
-    up, _ = spread(plugin_widening_factors[0], (state[0][1],))
+    own_chip(0, [])
     for tick in range(ticks):
         after = []
         if tick + 1 < ticks:
             begin(tick + 1)
             after.append(state[tick + 1][1])
+        near_chips(tick, after)
+        after = []
         if tick in returned:
             after.append(returned.pop(tick))
-        x, _, parts = state.pop(tick)
-        h = hs[tick] = layer(tick, parts, x, after)
+        x, _, _, parts = state.pop(tick)
+        h = layer_b(tick, parts, x, sums[tick], after)
         if tick + 1 < ticks:
-            state[tick + 1][2] = gather_end(state[tick + 1][2], [h])
+            own_chip(tick + 1, [h])
         onward = [(s, s + 1) for s in active(tick) if s + 1 < sections]
         if onward:
             arrived[tick + LAG] = lax.ppermute(h, "section", onward)
@@ -332,34 +391,38 @@
             if last % per_micro == per_micro - 1:
                 m = last // per_micro
                 block = [done[m * per_micro + b] for b in range(per_micro)]
-                if per_micro > 1:
-                    out_shape = pltpu.VMEM((rows, piece), jnp.bfloat16)
-                    block = call(join_kernel, out_shape, (info, *block), "join", 0, rows * piece * 4)
-                else:
-                    block = block[0]
                 home = m // batches_here
                 if home != sections - 1:
-                    block = lax.ppermute(block, "section", [(sections - 1, home)])
-                    returned[tick + 2] = block
+                    if per_micro > 1:
+                        out_shape = pltpu.VMEM((rows, piece), jnp.bfloat16)
+                        block = [call(join_kernel, out_shape, (info, *block), "join", 0, rows * piece * 4)]
+                    block = [lax.ppermute(block[0], "section", [(sections - 1, home)])]
+                    returned[tick + 2] = block[0]
                 home_blocks[m] = block
 
-    hidden, partial_score = [], []
+    hidden, scores = [], []
     for slot in range(batches_here):
+        blocks = [home_blocks[home * batches_here + slot] for home in range(sections)]
         out_shape = (
             jax.ShapeDtypeStruct((rows, piece), jnp.bfloat16),
-            jax.ShapeDtypeStruct((rows, 1), jnp.float32),
+            pltpu.VMEM((1, rows), jnp.float32),
         )
-        block = [home_blocks[home * batches_here + slot] for home in range(sections)]
-        kernel = functools.partial(finish_kernel, sections)
-        args = (info, *block, reward_head[None])
-        h, s = call(kernel, out_shape, args, "finish", 2 * rows * piece, rows * piece * 4)
+        kernel = functools.partial(finish_kernel, sections, [len(block) for block in blocks])
+        args = (info, *[part for block in blocks for part in block], reward_head[None])
+        h, score = call(kernel, out_shape, args, "finish", 2 * rows * piece, rows * piece * 4)
         hidden.append(h)
-        partial_score.append(s[:, 0])
-    raw = lax.psum(jnp.stack(partial_score), everyone)
-    place = jnp.arange(rows, dtype=jnp.int32) % BLOCK
-    limits = jnp.repeat(live_block_rows, BLOCK, axis=1)
-    scores = jnp.where(place[None, :] < limits, raw, jnp.float32(0.0))
-    return (jnp.stack(hidden), scores)
+        near_by = pltpu.VMEM((1, rows), jnp.float32)
+        if pairwise:
+            score = call(add_kernel, near_by, (info, score, *over_cores(score)), "add", 0, rows * 4)
+            terms = [score] + [over_chips(score, (k, k)) for k in (1, 2, 3)]
+        else:
+            terms = [lax.psum(score, everyone)]
+        limits = live_block_rows[slot : slot + 1]
+        out_shape = jax.ShapeDtypeStruct((1, rows), jnp.float32)
+        scores.append(call(score_kernel, out_shape, (info, limits, *terms), "score", 0, rows * 4))
+    if batches_here == 1:
+        return (hidden[0][None], scores[0])
+    return (jnp.stack(hidden), jnp.concatenate(scores, axis=0))
 
 
 def solution(mesh):

time: 316 us -> 330 us (1.044)
  Pallas kernels: 79.1 us -> 117 us
  waiting for transfers between devices: 106 us -> 87.5 us
  blocking collectives: 11.8 us -> 0 us
  starting transfers between devices: 114 us -> 121 us
    ppermute x42 -> x45, waiting for transfers between devices: 73.5 us -> 22 us  [over_chips(): return lax.ppermute(part, everyone, pairs)]
    pallas_call x37 -> x66, Pallas kernels: 73.2 us -> 111 us  [call(): pl.pallas_call(body, out_shape=out_shape, in_specs=[SMEM] + [VMEM] * coun...]
    ppermute x12, waiting for transfers between devices: 14.6 us -> 37.8 us  [shards(): arrived[tick + LAG] = lax.ppermute(h, 'section', onward)]
    psum x1 -> x0, blocking collectives: 11.8 us -> none  [shards(): raw = lax.psum(jnp.stack(partial_score), everyone)]
    ppermute x14, waiting for transfers between devices: 10.1 us -> 17.1 us  [spread(): lax.ppermute(blocks[k], everyone, [(i, i ^ k) for i in range(owners)])]
    ppermute x3, starting transfers between devices: 7 us -> 13.7 us  [shards(): lax.ppermute(block, 'section', [(home, 0)])]
    ppermute x56 -> x57, starting transfers between devices: 9.04 us -> 13.2 us  [over_cores(): lax.ppermute(part, 'core', [((c + k) % cores, c) for c in range(cores)])]
    ppermute x14, starting transfers between devices: 16.3 us -> 12.5 us  [spread(): lax.ppermute(blocks[k], everyone, [(i, i ^ k) for i in range(owners)])]
  transfers between devices with their start and end apart: 130 -> 134, of which waited for: 43 -> 33; matrix products, arithmetic and copies ran while one was open for 0% -> 0% of each run, Pallas kernels for 23% -> 33%
where the time goes in v1:
time: 330 us
  starting transfers between devices  121 us (37%)
  Pallas kernels  117 us (35%)
  waiting for transfers between devices  87.5 us (27%)
    pallas_call x66, Pallas kernels, call(): pl.pallas_call(body, out_shape=out_shape, in_specs=[SMEM] + [VMEM] * coun...  111 us
    ppermute x45, starting transfers between devices, over_chips(): return lax.ppermute(part, everyone, pairs)  45.8 us
    ppermute x12, waiting for transfers between devices, shards(): arrived[tick + LAG] = lax.ppermute(h, 'section', onward)  37.8 us
    ppermute x12, starting transfers between devices, shards(): arrived[tick + LAG] = lax.ppermute(h, 'section', onward)  32.7 us
    ppermute x45, waiting for transfers between devices, over_chips(): return lax.ppermute(part, everyone, pairs)  22 us
    ppermute x14, waiting for transfers between devices, spread(): lax.ppermute(blocks[k], everyone, [(i, i ^ k) for i in range(owners)])  17.1 us
    ppermute x3, starting transfers between devices, shards(): lax.ppermute(block, 'section', [(home, 0)])  13.7 us
    ppermute x57, starting transfers between devices, over_cores(): lax.ppermute(part, 'core', [((c + k) % cores, c) for c in range(cores)])  13.2 us
  transfers between devices with their start and end apart: 134, of which 33 were waited for; matrix products, arithmetic and copies ran while one was open for 0% of the time, Pallas kernels for 33%

profile of v1, /device:TPU:16, one launch (start us, length us, event | category | flops | bytes accessed | tf_op | source)
XLA Modules:
  0.0 329.6 jit_solution(17333184015068995567)
XLA Ops:
  11.2 5.8 %stage.1.refs_3_.refs_1_.refs_2_.refs_6_ = bf16[8192,1024]{1,0:T(8,128)(2,1)S(1)} custom-call(bf16[8192,1024]{1,0:T(8,128)(2,1)} %bitcast.23, bf16[1,64,1024]{2,1,0:T(8,128)(2,1)S(1)} %get-tuple-element.104.refs_0_), custom_call_target="tpu_custom_call" | custom-call | bytes 16777216 | tf_op jit(solution)/shard_map/stage/pallas_call | solution.py:101
  29.8 7.1 %collective-permute-done.14.refs_2_ = bf16[1,64,1024]{2,1,0:T(8,128)(2,1)S(1)} collective-permute-done((bf16[1,64,1024]{2,1,0:T(8,128)(2,1)S(1)}, bf16[1,64,1024]{2,1,0:T(8,128)(2,1)S(1)}, u32[]{:S(2)}, u32[]{:S(2)}) %collective-permute-start.14) | collective-permute-done | bytes 131104 | tf_op jit(solution)/shard_map/ppermute | solution.py:272
  47.0 5.3 %collective-permute-done.19.refs_7_ = bf16[1,64,1024]{2,1,0:T(8,128)(2,1)S(1)} collective-permute-done((bf16[1,64,1024]{2,1,0:T(8,128)(2,1)S(1)}, bf16[1,64,1024]{2,1,0:T(8,128)(2,1)S(1)}, u32[]{:S(2)}, u32[]{:S(2)}) %collective-permute-start.19) | collective-permute-done | bytes 131104 | tf_op jit(solution)/shard_map/ppermute | solution.py:272
  55.7 2.6 layer_a.29
  66.2 3.0 collective-permute-done.29.refs_0_
  70.8 2.6 layer_a.31
  81.7 3.7 %collective-permute-done.34.refs_0_ = bf16[1,128,1152]{2,1,0:T(8,128)(2,1)S(1)} collective-permute-done((bf16[1,128,1152]{2,1,0:T(8,128)(2,1)S(1)}, bf16[1,128,1152]{2,1,0:T(8,128)(2,1)S(1)}, u32[]{:S(2)}, u32[]{:S(2)}) %collective-permute-start.34) | collective-permute-done | bytes 294944 | tf_op jit(solution)/shard_map/ppermute | solution.py:292
  85.4 12.4 %collective-permute-start.1 = (bf16[256,1024]{1,0:T(8,128)(2,1)S(1)}, bf16[256,1024]{1,0:T(8,128)(2,1)S(1)}, u32[]{:S(2)}, u32[]{:S(2)}) collective-permute-start(bf16[256,1024]{1,0:T(8,128)(2,1)S(1)} %bitcast.19), channel_id=1, source_target_pairs={{16,0},{17,1},{18,2},{19,3},{20,4},{21,5},{22,6},{23,7}} | collective-permute-start | bytes 1572872 | tf_op jit(solution)/shard_map/ppermute | solution.py:283
  99.9 2.6 layer_a.33
  109.6 4.8 %collective-permute-done.40.refs_1_ = bf16[128,1024]{1,0:T(8,128)(2,1)S(1)} collective-permute-done((bf16[128,1024]{1,0:T(8,128)(2,1)S(1)}, bf16[128,1024]{1,0:T(8,128)(2,1)S(1)}, u32[]{:S(2)}, u32[]{:S(2)}) %collective-permute-start.40) | collective-permute-done | bytes 262176 | tf_op jit(solution)/shard_map/ppermute | solution.py:387
  118.3 2.6 layer_a.35
  126.7 5.9 %collective-permute-done.55.refs_1_ = bf16[128,1024]{1,0:T(8,128)(2,1)S(1)} collective-permute-done((bf16[128,1024]{1,0:T(8,128)(2,1)S(1)}, bf16[128,1024]{1,0:T(8,128)(2,1)S(1)}, u32[]{:S(2)}, u32[]{:S(2)}) %collective-permute-start.55) | collective-permute-done | bytes 262176 | tf_op jit(solution)/shard_map/ppermute | solution.py:387
  141.6 6.8 %collective-permute-start.56 = (bf16[128,1024]{1,0:T(8,128)(2,1)S(1)}, bf16[128,1024]{1,0:T(8,128)(2,1)S(1)}, u32[]{:S(2)}, u32[]{:S(2)}) collective-permute-start(bf16[128,1024]{1,0:T(8,128)(2,1)S(1)} %layer_b.18.refs_3_), channel_id=1, source_target_pairs={{0,8},{8,16},{16,24},{1,9},{9,17},{17,25},{2,10},{10,18},{18,26},{... | collective-permute-start | bytes 786440 | tf_op jit(solution)/shard_map/ppermute | solution.py:387
  150.8 2.9 collective-permute-done.56.refs_1_
  159.2 2.6 layer_a.39
  163.9 2.8 collective-permute-start.71
  169.1 4.9 %collective-permute-done.71.refs_1_ = bf16[128,1024]{1,0:T(8,128)(2,1)S(1)} collective-permute-done((bf16[128,1024]{1,0:T(8,128)(2,1)S(1)}, bf16[128,1024]{1,0:T(8,128)(2,1)S(1)}, u32[]{:S(2)}, u32[]{:S(2)}) %collective-permute-start.71) | collective-permute-done | bytes 262176 | tf_op jit(solution)/shard_map/ppermute | solution.py:387
  177.9 2.6 layer_a.41
  187.9 4.4 %collective-permute-done.79.refs_0_ = bf16[128,1024]{1,0:T(8,128)(2,1)S(1)} collective-permute-done((bf16[128,1024]{1,0:T(8,128)(2,1)S(1)}, bf16[128,1024]{1,0:T(8,128)(2,1)S(1)}, u32[]{:S(2)}, u32[]{:S(2)}) %collective-permute-start.79) | collective-permute-done | bytes 262176 | tf_op jit(solution)/shard_map/ppermute | solution.py:387
  196.2 2.6 layer_a.43
  206.2 4.4 %collective-permute-done.88.refs_0_ = bf16[128,1024]{1,0:T(8,128)(2,1)S(1)} collective-permute-done((bf16[128,1024]{1,0:T(8,128)(2,1)S(1)}, bf16[128,1024]{1,0:T(8,128)(2,1)S(1)}, u32[]{:S(2)}, u32[]{:S(2)}) %collective-permute-start.88) | collective-permute-done | bytes 262176 | tf_op jit(solution)/shard_map/ppermute | solution.py:387
  214.5 2.6 layer_a.45
  225.9 3.0 collective-permute-done.96.refs_0_
  232.4 2.6 layer_a.47
  237.1 6.1 %collective-permute-start.105 = (bf16[128,1024]{1,0:T(8,128)(2,1)S(1)}, bf16[128,1024]{1,0:T(8,128)(2,1)S(1)}, u32[]{:S(2)}, u32[]{:S(2)}) collective-permute-start(bf16[128,1024]{1,0:T(8,128)(2,1)S(1)} %layer_b.23.refs_1_.refs_3_), channel_id=1, source_target_pairs={{8,16},{16,24},{9,17},{17,25},{10,18},{18,26},{11,19},{19,27},{12,... | collective-permute-start | bytes 786440 | tf_op jit(solution)/shard_map/ppermute | solution.py:387
  249.3 2.6 collective-permute-done.100.refs_0_
  254.0 2.6 layer_a.49
  265.7 3.8 %collective-permute-done.113.refs_0_ = bf16[128,1024]{1,0:T(8,128)(2,1)S(1)} collective-permute-done((bf16[128,1024]{1,0:T(8,128)(2,1)S(1)}, bf16[128,1024]{1,0:T(8,128)(2,1)S(1)}, u32[]{:S(2)}, u32[]{:S(2)}) %collective-permute-start.113) | collective-permute-done | bytes 262176 | tf_op jit(solution)/shard_map/ppermute | solution.py:387
  271.3 2.6 layer_a.51
  277.6 4.4 %collective-permute-start.122 = (bf16[128,1024]{1,0:T(8,128)(2,1)S(1)}, bf16[128,1024]{1,0:T(8,128)(2,1)S(1)}, u32[]{:S(2)}, u32[]{:S(2)}) collective-permute-start(bf16[128,1024]{1,0:T(8,128)(2,1)S(1)} %layer_b.25.refs_1_.refs_3_), channel_id=1, source_target_pairs={{16,24},{17,25},{18,26},{19,27},{20,28},{21,29},{22,30},{23,31}} | collective-permute-start | bytes 786440 | tf_op jit(solution)/shard_map/ppermute | solution.py:387
  303.0 3.3 %collective-permute-done.125.refs_0_ = bf16[1,128,1152]{2,1,0:T(8,128)(2,1)S(1)} collective-permute-done((bf16[1,128,1152]{2,1,0:T(8,128)(2,1)S(1)}, bf16[1,128,1152]{2,1,0:T(8,128)(2,1)S(1)}, u32[]{:S(2)}, u32[]{:S(2)}) %collective-permute-start.125) | collective-permute-done | bytes 294944 | tf_op jit(solution)/shard_map/ppermute | solution.py:292
  308.9 7.1 %collective-permute-done.114.refs_7_.refs_2_ = bf16[256,1024]{1,0:T(8,128)(2,1)S(1)} collective-permute-done((bf16[256,1024]{1,0:T(8,128)(2,1)S(1)}, bf16[256,1024]{1,0:T(8,128)(2,1)S(1)}, u32[]{:S(2)}, u32[]{:S(2)}) %collective-permute-start.114) | collective-permute-done | bytes 524320 | tf_op jit(solution)/shard_map/ppermute | solution.py:399
  (332 shorter events, 194.5 us)
Async XLA Ops:
  5.1 11.9 %collective-permute-start.5 = (bf16[1,64,1024]{2,1,0:T(8,128)(2,1)S(1)}, bf16[1,64,1024]{2,1,0:T(8,128)(2,1)S(1)}, u32[]{:S(2)}, u32[]{:S(2)}) collective-permute-start(bf16[1,64,1024]{2,1,0:T(8,128)(2,1)S(1)} %get-tuple-element.107), channel_id=1, source_target_pairs={{0,3},{1,2},{2,1},{3,0},{4,7},{5,6},{6,5},{7,4},{8,11},{9,10},{10,... | collective-permute-start | bytes 393224 | tf_op jit(solution)/shard_map/ppermute | solution.py:272
  5.4 11.6 %collective-permute-start.6 = (bf16[1,64,1024]{2,1,0:T(8,128)(2,1)S(1)}, bf16[1,64,1024]{2,1,0:T(8,128)(2,1)S(1)}, u32[]{:S(2)}, u32[]{:S(2)}) collective-permute-start(bf16[1,64,1024]{2,1,0:T(8,128)(2,1)S(1)} %get-tuple-element.108), channel_id=1, source_target_pairs={{0,4},{1,5},{2,6},{3,7},{4,0},{5,1},{6,2},{7,3},{8,12},{9,13},{10,... | collective-permute-start | bytes 393224 | tf_op jit(solution)/shard_map/ppermute | solution.py:272
  6.9 12.1 %collective-permute-start.7 = (bf16[1,64,1024]{2,1,0:T(8,128)(2,1)S(1)}, bf16[1,64,1024]{2,1,0:T(8,128)(2,1)S(1)}, u32[]{:S(2)}, u32[]{:S(2)}) collective-permute-start(bf16[1,64,1024]{2,1,0:T(8,128)(2,1)S(1)} %get-tuple-element.109), channel_id=1, source_target_pairs={{0,5},{1,4},{2,7},{3,6},{4,1},{5,0},{6,3},{7,2},{8,13},{9,12},{10,... | collective-permute-start | bytes 393224 | tf_op jit(solution)/shard_map/ppermute | solution.py:272
  7.1 11.9 %collective-permute-start.8 = (bf16[1,64,1024]{2,1,0:T(8,128)(2,1)S(1)}, bf16[1,64,1024]{2,1,0:T(8,128)(2,1)S(1)}, u32[]{:S(2)}, u32[]{:S(2)}) collective-permute-start(bf16[1,64,1024]{2,1,0:T(8,128)(2,1)S(1)} %get-tuple-element.110), channel_id=1, source_target_pairs={{0,6},{1,7},{2,4},{3,5},{4,2},{5,3},{6,0},{7,1},{8,14},{9,15},{10,... | collective-permute-start | bytes 393224 | tf_op jit(solution)/shard_map/ppermute | solution.py:272
  22.4 22.0 %collective-permute-start.21 = (bf16[1,128,1152]{2,1,0:T(8,128)(2,1)S(1)}, bf16[1,128,1152]{2,1,0:T(8,128)(2,1)S(1)}, u32[]{:S(2)}, u32[]{:S(2)}) collective-permute-start(bf16[1,128,1152]{2,1,0:T(8,128)(2,1)S(1)} %collective-permute-done.20.refs_1_), channel_id=1, source_target_pairs={{0,2},{1,5},{2,0},{3,7},{4,6},{5,1},{6,4},{7,3},{8,10},{9,13},{10,... | collective-permute-start | bytes 884744 | tf_op jit(solution)/shard_map/ppermute | solution.py:292
  24.4 12.5 %collective-permute-start.14 = (bf16[1,64,1024]{2,1,0:T(8,128)(2,1)S(1)}, bf16[1,64,1024]{2,1,0:T(8,128)(2,1)S(1)}, u32[]{:S(2)}, u32[]{:S(2)}) collective-permute-start(bf16[1,64,1024]{2,1,0:T(8,128)(2,1)S(1)} %get-tuple-element.116), channel_id=1, source_target_pairs={{0,2},{1,3},{2,0},{3,1},{4,6},{5,7},{6,4},{7,5},{8,10},{9,11},{10,... | collective-permute-start | bytes 393224 | tf_op jit(solution)/shard_map/ppermute | solution.py:272
  25.9 12.7 %collective-permute-start.15 = (bf16[1,64,1024]{2,1,0:T(8,128)(2,1)S(1)}, bf16[1,64,1024]{2,1,0:T(8,128)(2,1)S(1)}, u32[]{:S(2)}, u32[]{:S(2)}) collective-permute-start(bf16[1,64,1024]{2,1,0:T(8,128)(2,1)S(1)} %get-tuple-element.117), channel_id=1, source_target_pairs={{0,3},{1,2},{2,1},{3,0},{4,7},{5,6},{6,5},{7,4},{8,11},{9,10},{10,... | collective-permute-start | bytes 393224 | tf_op jit(solution)/shard_map/ppermute | solution.py:272
  27.8 17.1 %collective-permute-start.11 = (bf16[1,128,1152]{2,1,0:T(8,128)(2,1)S(1)}, bf16[1,128,1152]{2,1,0:T(8,128)(2,1)S(1)}, u32[]{:S(2)}, u32[]{:S(2)}) collective-permute-start(bf16[1,128,1152]{2,1,0:T(8,128)(2,1)S(1)} %collective-permute-done.10.refs_0_), channel_id=1, source_target_pairs={{0,4},{1,3},{2,6},{3,1},{4,0},{5,7},{6,2},{7,5},{8,12},{9,11},{10,... | collective-permute-start | bytes 884744 | tf_op jit(solution)/shard_map/ppermute | solution.py:292
  29.3 13.5 %collective-permute-start.16 = (bf16[1,64,1024]{2,1,0:T(8,128)(2,1)S(1)}, bf16[1,64,1024]{2,1,0:T(8,128)(2,1)S(1)}, u32[]{:S(2)}, u32[]{:S(2)}) collective-permute-start(bf16[1,64,1024]{2,1,0:T(8,128)(2,1)S(1)} %get-tuple-element.118), channel_id=1, source_target_pairs={{0,4},{1,5},{2,6},{3,7},{4,0},{5,1},{6,2},{7,3},{8,12},{9,13},{10,... | collective-permute-start | bytes 393224 | tf_op jit(solution)/shard_map/ppermute | solution.py:272
  42.8 11.7 %collective-permute-start.22 = (bf16[1,128,1152]{2,1,0:T(8,128)(2,1)S(1)}, bf16[1,128,1152]{2,1,0:T(8,128)(2,1)S(1)}, u32[]{:S(2)}, u32[]{:S(2)}) collective-permute-start(bf16[1,128,1152]{2,1,0:T(8,128)(2,1)S(1)} %collective-permute-done.10.refs_0_), channel_id=1, source_target_pairs={{1,0},{0,1},{3,2},{2,3},{5,4},{4,5},{7,6},{6,7},{9,8},{8,9},{11,10... | collective-permute-start | bytes 884744 | tf_op jit(solution)/shard_map/ppermute | solution.py:287
  44.9 13.4 %collective-permute-start.12 = (bf16[1,128,1152]{2,1,0:T(8,128)(2,1)S(1)}, bf16[1,128,1152]{2,1,0:T(8,128)(2,1)S(1)}, u32[]{:S(2)}, u32[]{:S(2)}) collective-permute-start(bf16[1,128,1152]{2,1,0:T(8,128)(2,1)S(1)} %collective-permute-done.11.refs_0_), channel_id=1, source_target_pairs={{1,0},{0,1},{3,2},{2,3},{5,4},{4,5},{7,6},{6,7},{9,8},{8,9},{11,10... | collective-permute-start | bytes 884744 | tf_op jit(solution)/shard_map/ppermute | solution.py:287
  80.2 17.6 %collective-permute-start.37 = (bf16[1,128,1152]{2,1,0:T(8,128)(2,1)S(1)}, bf16[1,128,1152]{2,1,0:T(8,128)(2,1)S(1)}, u32[]{:S(2)}, u32[]{:S(2)}) collective-permute-start(bf16[1,128,1152]{2,1,0:T(8,128)(2,1)S(1)} %tie.14.refs_0_), channel_id=1, source_target_pairs={{1,0},{0,1},{3,2},{2,3},{5,4},{4,5},{7,6},{6,7},{9,8},{8,9},{11,10... | collective-permute-start | bytes 884744 | tf_op jit(solution)/shard_map/ppermute | solution.py:287
  81.0 17.1 %collective-permute-start.41 = (bf16[1,128,1152]{2,1,0:T(8,128)(2,1)S(1)}, bf16[1,128,1152]{2,1,0:T(8,128)(2,1)S(1)}, u32[]{:S(2)}, u32[]{:S(2)}) collective-permute-start(bf16[1,128,1152]{2,1,0:T(8,128)(2,1)S(1)} %get-tuple-element.136.refs_7_.refs_0_), channel_id=1, source_target_pairs={{1,0},{0,1},{3,2},{2,3},{5,4},{4,5},{7,6},{6,7},{9,8},{8,9},{11,10... | collective-permute-start | bytes 884744 | tf_op jit(solution)/shard_map/ppermute | solution.py:287
  81.6 18.3 %collective-permute-start.38 = (bf16[1,128,1152]{2,1,0:T(8,128)(2,1)S(1)}, bf16[1,128,1152]{2,1,0:T(8,128)(2,1)S(1)}, u32[]{:S(2)}, u32[]{:S(2)}) collective-permute-start(bf16[1,128,1152]{2,1,0:T(8,128)(2,1)S(1)} %collective-permute-done.36.refs_1_), channel_id=1, source_target_pairs={{1,0},{0,1},{3,2},{2,3},{5,4},{4,5},{7,6},{6,7},{9,8},{8,9},{11,10... | collective-permute-start | bytes 884744 | tf_op jit(solution)/shard_map/ppermute | solution.py:287
  85.4 17.1 %collective-permute-start.35 = (bf16[1,128,1152]{2,1,0:T(8,128)(2,1)S(1)}, bf16[1,128,1152]{2,1,0:T(8,128)(2,1)S(1)}, u32[]{:S(2)}, u32[]{:S(2)}) collective-permute-start(bf16[1,128,1152]{2,1,0:T(8,128)(2,1)S(1)} %collective-permute-done.34.refs_0_), channel_id=1, source_target_pairs={{1,0},{0,1},{3,2},{2,3},{5,4},{4,5},{7,6},{6,7},{9,8},{8,9},{11,10... | collective-permute-start | bytes 884744 | tf_op jit(solution)/shard_map/ppermute | solution.py:287
  85.4 24.2 %collective-permute-start.1 = (bf16[256,1024]{1,0:T(8,128)(2,1)S(1)}, bf16[256,1024]{1,0:T(8,128)(2,1)S(1)}, u32[]{:S(2)}, u32[]{:S(2)}) collective-permute-start(bf16[256,1024]{1,0:T(8,128)(2,1)S(1)} %bitcast.19), channel_id=1, source_target_pairs={{16,0},{17,1},{18,2},{19,3},{20,4},{21,5},{22,6},{23,7}} | collective-permute-start | bytes 1572872 | tf_op jit(solution)/shard_map/ppermute | solution.py:283
  98.1 17.6 %collective-permute-start.47 = (bf16[1,128,1152]{2,1,0:T(8,128)(2,1)S(1)}, bf16[1,128,1152]{2,1,0:T(8,128)(2,1)S(1)}, u32[]{:S(2)}, u32[]{:S(2)}) collective-permute-start(bf16[1,128,1152]{2,1,0:T(8,128)(2,1)S(1)} %collective-permute-done.41.refs_1_), channel_id=1, source_target_pairs={{0,2},{1,5},{2,0},{3,7},{4,6},{5,1},{6,4},{7,3},{8,10},{9,13},{10,... | collective-permute-start | bytes 884744 | tf_op jit(solution)/shard_map/ppermute | solution.py:292
  116.8 16.7 %collective-permute-start.52 = (bf16[1,128,1152]{2,1,0:T(8,128)(2,1)S(1)}, bf16[1,128,1152]{2,1,0:T(8,128)(2,1)S(1)}, u32[]{:S(2)}, u32[]{:S(2)}) collective-permute-start(bf16[1,128,1152]{2,1,0:T(8,128)(2,1)S(1)} %collective-permute-done.43.refs_1_), channel_id=1, source_target_pairs={{0,2},{1,5},{2,0},{3,7},{4,6},{5,1},{6,4},{7,3},{8,10},{9,13},{10,... | collective-permute-start | bytes 884744 | tf_op jit(solution)/shard_map/ppermute | solution.py:292
  134.1 16.7 %collective-permute-start = (bf16[256,1024]{1,0:T(8,128)(2,1)S(1)}, bf16[256,1024]{1,0:T(8,128)(2,1)S(1)}, u32[]{:S(2)}, u32[]{:S(2)}) collective-permute-start(bf16[256,1024]{1,0:T(8,128)(2,1)S(1)} %bitcast.20), channel_id=1, source_target_pairs={{24,0},{25,1},{26,2},{27,3},{28,4},{29,5},{30,6},{31,7}} | collective-permute-start | bytes 1572872 | tf_op jit(solution)/shard_map/ppermute | solution.py:283
  134.8 15.6 %collective-permute-start.60 = (bf16[1,128,1152]{2,1,0:T(8,128)(2,1)S(1)}, bf16[1,128,1152]{2,1,0:T(8,128)(2,1)S(1)}, u32[]{:S(2)}, u32[]{:S(2)}) collective-permute-start(bf16[1,128,1152]{2,1,0:T(8,128)(2,1)S(1)} %get-tuple-element.148.refs_7_.refs_0_), channel_id=1, source_target_pairs={{0,2},{1,5},{2,0},{3,7},{4,6},{5,1},{6,4},{7,3},{8,10},{9,13},{10,... | collective-permute-start | bytes 884744 | tf_op jit(solution)/shard_map/ppermute | solution.py:292
  135.5 19.6 %collective-permute-start.63 = (bf16[1,128,1152]{2,1,0:T(8,128)(2,1)S(1)}, bf16[1,128,1152]{2,1,0:T(8,128)(2,1)S(1)}, u32[]{:S(2)}, u32[]{:S(2)}) collective-permute-start(bf16[1,128,1152]{2,1,0:T(8,128)(2,1)S(1)} %collective-permute-done.57.refs_1_), channel_id=1, source_target_pairs={{0,2},{1,5},{2,0},{3,7},{4,6},{5,1},{6,4},{7,3},{8,10},{9,13},{10,... | collective-permute-start | bytes 884744 | tf_op jit(solution)/shard_map/ppermute | solution.py:292
  141.6 12.1 %collective-permute-start.56 = (bf16[128,1024]{1,0:T(8,128)(2,1)S(1)}, bf16[128,1024]{1,0:T(8,128)(2,1)S(1)}, u32[]{:S(2)}, u32[]{:S(2)}) collective-permute-start(bf16[128,1024]{1,0:T(8,128)(2,1)S(1)} %layer_b.18.refs_3_), channel_id=1, source_target_pairs={{0,8},{8,16},{16,24},{1,9},{9,17},{17,25},{2,10},{10,18},{18,26},{... | collective-permute-start | bytes 786440 | tf_op jit(solution)/shard_map/ppermute | solution.py:387
  157.5 17.9 %collective-permute-start.68 = (bf16[1,128,1152]{2,1,0:T(8,128)(2,1)S(1)}, bf16[1,128,1152]{2,1,0:T(8,128)(2,1)S(1)}, u32[]{:S(2)}, u32[]{:S(2)}) collective-permute-start(bf16[1,128,1152]{2,1,0:T(8,128)(2,1)S(1)} %collective-permute-done.59.refs_1_), channel_id=1, source_target_pairs={{0,2},{1,5},{2,0},{3,7},{4,6},{5,1},{6,4},{7,3},{8,10},{9,13},{10,... | collective-permute-start | bytes 884744 | tf_op jit(solution)/shard_map/ppermute | solution.py:292
  176.5 17.2 %collective-permute-start.76 = (bf16[1,128,1152]{2,1,0:T(8,128)(2,1)S(1)}, bf16[1,128,1152]{2,1,0:T(8,128)(2,1)S(1)}, u32[]{:S(2)}, u32[]{:S(2)}) collective-permute-start(bf16[1,128,1152]{2,1,0:T(8,128)(2,1)S(1)} %collective-permute-done.73.refs_1_), channel_id=1, source_target_pairs={{0,2},{1,5},{2,0},{3,7},{4,6},{5,1},{6,4},{7,3},{8,10},{9,13},{10,... | collective-permute-start | bytes 884744 | tf_op jit(solution)/shard_map/ppermute | solution.py:292
  194.8 17.1 %collective-permute-start.85 = (bf16[1,128,1152]{2,1,0:T(8,128)(2,1)S(1)}, bf16[1,128,1152]{2,1,0:T(8,128)(2,1)S(1)}, u32[]{:S(2)}, u32[]{:S(2)}) collective-permute-start(bf16[1,128,1152]{2,1,0:T(8,128)(2,1)S(1)} %collective-permute-done.82.refs_1_), channel_id=1, source_target_pairs={{0,2},{1,5},{2,0},{3,7},{4,6},{5,1},{6,4},{7,3},{8,10},{9,13},{10,... | collective-permute-start | bytes 884744 | tf_op jit(solution)/shard_map/ppermute | solution.py:292
  213.1 16.6 %collective-permute-start.93 = (bf16[1,128,1152]{2,1,0:T(8,128)(2,1)S(1)}, bf16[1,128,1152]{2,1,0:T(8,128)(2,1)S(1)}, u32[]{:S(2)}, u32[]{:S(2)}) collective-permute-start(bf16[1,128,1152]{2,1,0:T(8,128)(2,1)S(1)} %collective-permute-done.90.refs_1_), channel_id=1, source_target_pairs={{0,2},{1,5},{2,0},{3,7},{4,6},{5,1},{6,4},{7,3},{8,10},{9,13},{10,... | collective-permute-start | bytes 884744 | tf_op jit(solution)/shard_map/ppermute | solution.py:292
  230.3 14.8 %collective-permute-start.98 = (bf16[1,128,1152]{2,1,0:T(8,128)(2,1)S(1)}, bf16[1,128,1152]{2,1,0:T(8,128)(2,1)S(1)}, u32[]{:S(2)}, u32[]{:S(2)}) collective-permute-start(bf16[1,128,1152]{2,1,0:T(8,128)(2,1)S(1)} %get-tuple-element.178.refs_7_.refs_0_), channel_id=1, source_target_pairs={{0,2},{1,5},{2,0},{3,7},{4,6},{5,1},{6,4},{7,3},{8,10},{9,13},{10,... | collective-permute-start | bytes 884744 | tf_op jit(solution)/shard_map/ppermute | solution.py:292
  231.3 18.0 %collective-permute-start.102 = (bf16[1,128,1152]{2,1,0:T(8,128)(2,1)S(1)}, bf16[1,128,1152]{2,1,0:T(8,128)(2,1)S(1)}, u32[]{:S(2)}, u32[]{:S(2)}) collective-permute-start(bf16[1,128,1152]{2,1,0:T(8,128)(2,1)S(1)} %collective-permute-done.99.refs_1_), channel_id=1, source_target_pairs={{0,2},{1,5},{2,0},{3,7},{4,6},{5,1},{6,4},{7,3},{8,10},{9,13},{10,... | collective-permute-start | bytes 884744 | tf_op jit(solution)/shard_map/ppermute | solution.py:292
  253.4 11.7 %collective-permute-start.110 = (bf16[1,128,1152]{2,1,0:T(8,128)(2,1)S(1)}, bf16[1,128,1152]{2,1,0:T(8,128)(2,1)S(1)}, u32[]{:S(2)}, u32[]{:S(2)}) collective-permute-start(bf16[1,128,1152]{2,1,0:T(8,128)(2,1)S(1)} %collective-permute-done.107.refs_1_), channel_id=1, source_target_pairs={{0,2},{1,5},{2,0},{3,7},{4,6},{5,1},{6,4},{7,3},{8,10},{9,13},{10,... | collective-permute-start | bytes 884744 | tf_op jit(solution)/shard_map/ppermute | solution.py:292
  270.9 13.2 %collective-permute-start.115 = (bf16[1,128,1152]{2,1,0:T(8,128)(2,1)S(1)}, bf16[1,128,1152]{2,1,0:T(8,128)(2,1)S(1)}, u32[]{:S(2)}, u32[]{:S(2)}) collective-permute-start(bf16[1,128,1152]{2,1,0:T(8,128)(2,1)S(1)} %get-tuple-element.190.refs_7_.refs_0_), channel_id=1, source_target_pairs={{0,2},{1,5},{2,0},{3,7},{4,6},{5,1},{6,4},{7,3},{8,10},{9,13},{10,... | collective-permute-start | bytes 884744 | tf_op jit(solution)/shard_map/ppermute | solution.py:292
  273.9 14.8 %collective-permute-start.119 = (bf16[1,128,1152]{2,1,0:T(8,128)(2,1)S(1)}, bf16[1,128,1152]{2,1,0:T(8,128)(2,1)S(1)}, u32[]{:S(2)}, u32[]{:S(2)}) collective-permute-start(bf16[1,128,1152]{2,1,0:T(8,128)(2,1)S(1)} %collective-permute-done.116.refs_1_), channel_id=1, source_target_pairs={{0,2},{1,5},{2,0},{3,7},{4,6},{5,1},{6,4},{7,3},{8,10},{9,13},{10,... | collective-permute-start | bytes 884744 | tf_op jit(solution)/shard_map/ppermute | solution.py:292
  301.1 14.9 %collective-permute-start.114 = (bf16[256,1024]{1,0:T(8,128)(2,1)S(1)}, bf16[256,1024]{1,0:T(8,128)(2,1)S(1)}, u32[]{:S(2)}, u32[]{:S(2)}) collective-permute-start(bf16[256,1024]{1,0:T(8,128)(2,1)S(1)} %join.5), channel_id=1, source_target_pairs={{24,16},{25,17},{26,18},{27,19},{28,20},{29,21},{30,22},{31,23}} | collective-permute-start | bytes 1572872 | tf_op jit(solution)/shard_map/ppermute | solution.py:399
  (108 other events, 691.3 us)
